TPU v7x, 256 devices: a whole 4x4x8 slice. The times are simulated.
256 devices in a mesh: dp: 32 (over y, z), tensor: 8 (over x, core).
Axes of the slice: x: 4, y: 4, z: 8, core: 2. Of those that a mesh axis runs over, the one named last changes fastest.
Arguments:
- hidden: bfloat16 [512, 256, 768], P(('dp', 'tensor')), may hold values from -64 to 64
- lengths: int32 [512], P('dp'), may hold values from 64 to 256, as said below
- owner_of: int32 [512, 1], P('dp'), may hold values from 0 to 31; in each aligned block of 16 rows (0 to 15, 16 to 31, ...) at most 2 rows name the same one
- list_local: int32 [512], P('dp'), may hold values from 0 to 1023
- old_weight: int32 [32768], P('dp'), may hold values from 1 to 8
- old_centroids: float32 [32768, 768], P('dp'), may hold values from -6 to 6
- w_qkv: bfloat16 [768, 2304], P('dp'), may hold values from -0.21875 to 0.21875
- w_out: bfloat16 [768, 768], P('dp'), may hold values from -0.21875 to 0.21875
- gain_one: float32 [768], replicated, may hold values from 0.1 to 1.9
- shift_one: float32 [768], replicated, may hold values from -2 to 2
- w_up: bfloat16 [768, 3072], P('dp', 'tensor'), may hold values from -0.21875 to 0.21875
- w_down: bfloat16 [3072, 768], P('tensor', 'dp'), may hold values from -0.109375 to 0.109375
- gain_two: float32 [768], replicated, may hold values from 0.1 to 1.9
- shift_two: float32 [768], replicated, may hold values from -2 to 2
- rotation: float32 [768, 768], P('tensor'), may hold values from -0.21875 to 0.21875
Outputs:
- rotated: float32 [512, 768], P('dp', 'tensor')
- centroids: float32 [32768, 768], P('dp')
Inputs may be any that keep to these rules, and one draw needn't show every extreme that they name: `lengths`: some passage has 256 tokens in every draw. `owner_of`: among the passages of one index of dp, at most 2 name the same owner.
All inputs are finite; a program needn't handle non-finite values.
Results may differ from a plain program's by a relative error of at most 0.003.
Values may be sent and summed in bfloat16 or wider, within the bound.
A program may use at most 64 MiB of HBM per device.

v0:
```python
import jax
import jax.numpy as jnp
from jax import lax
from jax.sharding import PartitionSpec as P

HEADS = 12
HEAD_DIM = 64


EPS = 1e-05


def norm_rows(values, gain, shift):
    mean = jnp.mean(values, axis=-1, keepdims=True)
    centered = values - mean
    spread = jnp.mean(centered * centered, axis=-1, keepdims=True)
    return centered * lax.rsqrt(spread + EPS) * gain + shift


def pool_valid(states, lens):
    width = states.shape[1]
    tok_ok = jnp.arange(width)[None, :] < lens[:, None]
    summed = jnp.sum(jnp.where(tok_ok[:, :, None], states, 0.0), axis=1)
    return summed / lens[:, None].astype(jnp.float32)


def local(
    hidden,
    lengths,
    owner_of,
    list_local,
    old_weight,
    old_centroids,
    w_qkv,
    w_out,
    gain_one,
    shift_one,
    w_up,
    w_down,
    gain_two,
    shift_two,
    rotation,
):
    count, slots_len, width = hidden.shape
    rows = count * slots_len
    tens = lax.axis_index("tensor")
    my_lens = lax.dynamic_slice_in_dim(lengths, tens * count, count)
    flat = hidden.reshape(rows, width)
    cols = flat
    qkv = jnp.dot(
        cols, lax.all_gather(w_qkv, "dp", axis=0, tiled=True), preferred_element_type=jnp.float32
    )
    qkv = qkv.astype(jnp.bfloat16).reshape(count, slots_len, 3, HEADS, HEAD_DIM)
    scores = jnp.einsum(
        "plhe,pmhe->phlm", qkv[:, :, 0], qkv[:, :, 1], preferred_element_type=jnp.float32
    ) * HEAD_DIM ** (-0.5)
    keys_ok = jnp.arange(slots_len)[None, None, None, :] < my_lens[:, None, None, None]
    scores = jnp.where(keys_ok, scores, -1e30)
    probs = jax.nn.softmax(scores, axis=-1).astype(jnp.bfloat16)
    context = jnp.einsum("phlm,pmhe->plhe", probs, qkv[:, :, 2], preferred_element_type=jnp.float32)
    context = context.astype(jnp.bfloat16).reshape(rows, width)
    cols = context
    mixed = jnp.dot(
        cols, lax.all_gather(w_out, "dp", axis=0, tiled=True), preferred_element_type=jnp.float32
    )
    first = norm_rows(flat.astype(jnp.float32) + mixed, gain_one, shift_one).astype(jnp.bfloat16)
    up_full, down_full = (
        lax.all_gather(w_up, "dp", axis=0, tiled=True),
        lax.all_gather(w_down, "dp", axis=1, tiled=True),
    )
    n_tens = lax.axis_size("tensor")
    group = count * n_tens
    feat = width // n_tens
    leader = (tens == 0).astype(jnp.float32)
    piece = lax.all_gather(first, "tensor", axis=0, tiled=True)
    act = jax.nn.gelu(
        jnp.dot(piece, up_full, preferred_element_type=jnp.float32), approximate=False
    ).astype(jnp.bfloat16)
    terms = jnp.dot(act, down_full, preferred_element_type=jnp.float32) + leader * piece.astype(
        jnp.float32
    )
    total = lax.psum_scatter(
        terms.astype(jnp.bfloat16), "tensor", scatter_dimension=0, tiled=True
    ).astype(jnp.float32)
    second = norm_rows(total, gain_two, shift_two).reshape(count, slots_len, width)
    pooled = pool_valid(second, my_lens)
    emb = lax.all_to_all(pooled, "tensor", split_axis=1, concat_axis=0, tiled=True)
    n_owners = lax.axis_size("dp")
    capacity = max(2, 2 * group // n_owners)
    slot_total = n_owners * capacity
    owner = owner_of[:, 0]
    places = jnp.arange(group)
    earlier = (owner[:, None] == owner[None, :]) & (places[None, :] < places[:, None])
    rank = jnp.sum(earlier.astype(jnp.int32), axis=1)
    slot = owner * capacity + rank
    placed = slot[None, :] == jnp.arange(slot_total)[:, None]
    send_emb = jnp.dot(placed.astype(jnp.float32), emb, precision=lax.Precision.HIGHEST)
    send_list = jnp.max(jnp.where(placed, list_local[None, :], -1), axis=1)
    recv_emb, recv_list = (
        lax.all_to_all(send_emb, "dp", split_axis=0, concat_axis=0, tiled=True),
        lax.all_to_all(send_list, "dp", split_axis=0, concat_axis=0, tiled=True),
    )
    recv_vals = lax.all_gather(recv_emb, "tensor", axis=1, tiled=True)
    owned = old_weight.shape[0]
    list_hot = (recv_list[:, None] == jnp.arange(owned)[None, :]).astype(jnp.float32)
    sums = lax.dot_general(
        list_hot, recv_vals, (((0,), (0,)), ((), ())), precision=lax.Precision.HIGHEST
    )
    counts = jnp.sum(list_hot, axis=0)
    weight = old_weight.astype(jnp.float32)
    centroids = (weight[:, None] * old_centroids + sums) / (weight + counts)[:, None]
    resid = recv_vals - jnp.dot(list_hot, centroids, precision=lax.Precision.HIGHEST)
    resid_part = lax.dynamic_slice_in_dim(resid, tens * feat, feat, 1)
    returned = lax.all_to_all(resid_part, "dp", split_axis=0, concat_axis=0, tiled=True)
    mine = lax.dot_general(
        placed.astype(jnp.float32),
        returned,
        (((0,), (0,)), ((), ())),
        precision=lax.Precision.HIGHEST,
    )
    partial_rot = jnp.dot(mine, rotation, precision=lax.Precision.HIGHEST)
    rotated = lax.psum_scatter(partial_rot, "tensor", scatter_dimension=1, tiled=True)
    return (rotated, centroids)


def solution(mesh):
    return jax.shard_map(
        local,
        mesh=mesh,
        in_specs=(
            P(("dp", "tensor"), None, None),
            P("dp"),
            P("dp", None),
            P("dp"),
            P("dp"),
            P("dp", None),
            P("dp", None),
            P("dp", None),
            P(),
            P(),
            P("dp", "tensor"),
            P("tensor", "dp"),
            P(),
            P(),
            P("tensor", None),
        ),
        out_specs=(P("dp", "tensor"), P("dp", None)),
        check_vma=False,
    )
```

profile of v0, /device:TPU:1, one launch (start us, length us, event | category | flops | bytes accessed | tf_op | source)
XLA Modules:
  0.0 438.5 jit_solution(2842044659153720166)
XLA Ops:
  7.2 0.7 all-gather.5.cloned.1.call-update
  8.0 0.7 all-gather.7.cloned.1.call-update
  8.7 0.7 fusion.97
  9.5 82.2 %all-gather.5.cloned.1.call-done = bf16[768,2304]{1,0:T(8,128)(2,1)} async-done(((bf16[24,2304]{1,0:T(8,128)(2,1)}), bf16[768,2304]{1,0:T(8,128)(2,1)}) %all-gather.5.cloned.1.call-update) | async-done | bytes 3538960 | tf_op jit(solution)/shard_map/all_gather | solution.py:51
  91.7 4.2 convolution_convert_fusion
  96.0 2.4 copy.40
  98.4 5.0 %reshape.138 = bf16[2,256,3,12,64]{1,0,4,3,2:T(2,128)(2,1)S(1)} reshape(bf16[512,2304]{0,1:T(8,128)(2,1)} %copy.40) | data formatting | bytes 4718592 | tf_op jit(solution)/shard_map/reshape | solution.py:53
  103.4 1.7 fusion.98
  105.1 1.0 fusion.54
  106.1 2.8 fusion.99
  108.9 0.6 fusion.53
  109.5 0.8 copy.45
  110.4 0.2 copy.56
  110.5 56.2 %all-gather.7.cloned.1.call-done = bf16[768,768]{1,0:T(8,128)(2,1)} async-done(((bf16[24,768]{1,0:T(8,128)(2,1)}), bf16[768,768]{1,0:T(8,128)(2,1)}) %all-gather.7.cloned.1.call-update) | async-done | bytes 1179664 | tf_op jit(solution)/shard_map/all_gather | solution.py:64
  166.7 2.2 fusion.100
  168.9 0.3 multiply_reduce_fusion
  169.2 1.2 add_convert_fusion.1
  170.5 38.5 %all_gather.21 = bf16[768,384]{1,0:T(8,128)(2,1)S(1)} all-gather(bf16[24,384]{1,0:T(8,128)(2,1)S(1)} %copy-done.2), channel_id=1, replica_groups=mesh['dp'=32,'tensor'=8] {'dp'}, dimensions={0}, use_global_device_ids=true | all-gather | bytes 608256 | tf_op jit(solution)/shard_map/all_gather | solution.py:68
  209.0 37.3 %all_gather.22 = bf16[384,768]{0,1:T(8,128)(2,1)S(1)} all-gather(bf16[384,24]{0,1:T(8,128)(2,1)S(1)} %copy-done.3), channel_id=1, replica_groups=mesh['dp'=32,'tensor'=8] {'dp'}, dimensions={1}, use_global_device_ids=true | all-gather | bytes 608256 | tf_op jit(solution)/shard_map/all_gather | solution.py:69
  246.3 23.0 %add_convert_fusion = bf16[4096,768]{1,0:T(8,128)(2,1)} fusion(bf16[4096,768]{1,0:T(8,128)(2,1)} %all-gather.9.cloned.1.call-done, bf16[384,768]{0,1:T(8,128)(2,1)S(1)} %all_gather.22, f32[]{:T(128)S(6)} %convert_element_type.56, bf16[768,384]{1,0:T(8,128)(2,1)S(1)} %all_gather.21), kind=kOutput, calls=%fused_computation.1 | convolution fusion | flops 4946657280 | bytes 13762564 | tf_op jit(solution)/shard_map/dot_general | solution.py:79
  269.4 0.6 copy-done.10
  270.0 0.2 convert_reduce_fusion.2
  270.3 0.7 all_to_all.37
  271.0 5.4 %all-to-all-start.2 = ((s32[32,2,1]{1,2,0:T(1,128)}), s32[32,2,1]{1,2,0:T(1,128)S(1)}, u32[]{:S(2)}, u32[]{:S(2)}) async-start(s32[32,2,1]{1,2,0:T(1,128)} %bitcast.14), calls=%async_computation.3 | async-start | bytes 32768 | tf_op jit(solution)/shard_map/all_to_all | solution.py:101
  276.4 8.5 %all-to-all-done.2 = s32[32,2,1]{1,2,0:T(1,128)S(1)} async-done(((s32[32,2,1]{1,2,0:T(1,128)}), s32[32,2,1]{1,2,0:T(1,128)S(1)}, u32[]{:S(2)}, u32[]{:S(2)}) %all-to-all-start.2) | async-done | bytes 288 | tf_op jit(solution)/shard_map/all_to_all | solution.py:101
  285.0 0.5 broadcast.127
  285.5 0.7 reduce.3
  286.3 50.5 %reduce-scatter.5.cloned.1.call-done = bf16[512,768]{1,0:T(8,128)(2,1)} async-done(((bf16[4096,768]{1,0:T(8,128)(2,1)}), bf16[512,768]{1,0:T(8,128)(2,1)}) %reduce-scatter.5.cloned.1.call-update) | async-done | bytes 786448 | tf_op jit(solution)/shard_map/reduce_scatter | solution.py:82
  336.8 1.3 convert_reduce_fusion
  338.1 1.5 fusion.49
  339.6 1.6 select_reduce_fusion
  341.4 0.6 copy.46
  342.0 4.5 %all-to-all-start = ((f32[2,8,96]{2,0,1:T(2,128)}), f32[2,8,96]{2,0,1:T(2,128)S(1)}, u32[]{:S(2)}, u32[]{:S(2)}) async-start(f32[2,8,96]{2,0,1:T(2,128)} %copy.46), calls=%async_computation.1 | async-start | bytes 16384 | tf_op jit(solution)/shard_map/all_to_all | solution.py:87
  346.6 4.5 %all-to-all-done = f32[2,8,96]{2,0,1:T(2,128)S(1)} async-done(((f32[2,8,96]{2,0,1:T(2,128)}), f32[2,8,96]{2,0,1:T(2,128)S(1)}, u32[]{:S(2)}, u32[]{:S(2)}) %all-to-all-start) | async-done | bytes 6176 | tf_op jit(solution)/shard_map/all_to_all | solution.py:87
  351.1 0.3 fusion.58
  351.4 0.6 copy.47
  352.0 9.6 %all-to-all-start.1 = ((f32[32,2,96]{2,1,0:T(2,128)}), f32[32,2,96]{2,1,0:T(2,128)S(1)}, u32[]{:S(2)}, u32[]{:S(2)}) async-start(f32[32,2,96]{2,1,0:T(2,128)} %copy.47), calls=%async_computation.2 | async-start | bytes 65536 | tf_op jit(solution)/shard_map/all_to_all | solution.py:100
  361.7 8.7 %all-to-all-done.1 = f32[32,2,96]{2,1,0:T(2,128)S(1)} async-done(((f32[32,2,96]{2,1,0:T(2,128)}), f32[32,2,96]{2,1,0:T(2,128)S(1)}, u32[]{:S(2)}, u32[]{:S(2)}) %all-to-all-start.1) | async-done | bytes 24608 | tf_op jit(solution)/shard_map/all_to_all | solution.py:100
  370.4 14.8 %all-gather = f32[8,96,64]{1,2,0:T(8,128)S(1)} all-gather(f32[1,96,64]{1,2,0:T(8,128)S(1)} %bitcast.59), channel_id=1, replica_groups=mesh['dp'=32,'tensor'=8] {'tensor'}, dimensions={0}, use_global_device_ids=true | all-gather | bytes 221184 | tf_op jit(solution)/shard_map/all_gather | solution.py:103
  385.3 0.8 reshape.142
  386.1 3.8 add_divide_fusion
  389.9 1.4 fusion.55
  391.3 0.9 dynamic-slice_subtract_fusion
  392.2 11.7 %all_to_all.46 = f32[32,2,96]{2,1,0:T(2,128)S(1)} all-to-all(f32[32,2,96]{2,1,0:T(2,128)S(1)} %bitcast.60), channel_id=1, replica_groups=mesh['dp'=32,'tensor'=8] {'dp'}, dimensions={0} | all-to-all | bytes 49152 | tf_op jit(solution)/shard_map/all_to_all | solution.py:114
  403.9 0.2 fusion.61
  404.1 1.6 convolution_bitcast_fusion
  405.7 24.8 %reduce-scatter.7.cloned.1.call-done = f32[96,16]{1,0:T(8,128)} async-done(((f32[768,16]{1,0:T(8,128)}), f32[96,16]{1,0:T(8,128)}) %reduce-scatter.7.cloned.1.call-update) | async-done | bytes 6160
  430.5 1.5 copy.52
  (47 shorter events, 1.0 us)
Async XLA Ops:
  7.2 396.9 %copy-start = (f32[96,768]{1,0:T(8,128)S(1)}, f32[96,768]{1,0:T(8,128)}, u32[]{:S(2)}) copy-start(f32[96,768]{1,0:T(8,128)} %param.29) | copy-start | bytes 884740
  7.2 84.5 %all-gather.5.cloned.1.call-start = ((), (), s32[]{:S(2)}) async-start(), calls=%async_computation.6 | async-start | bytes 3649536 | tf_op jit(solution)/shard_map/all_gather | solution.py:51
  7.9 158.8 %all-gather.7.cloned.1.call-start = ((), (), s32[]{:S(2)}) async-start(), calls=%async_computation.7 | async-start | bytes 1216512 | tf_op jit(solution)/shard_map/all_gather | solution.py:64
  8.7 237.7 %all-gather.9.cloned.1.call-start = ((), (), s32[]{:S(2)}) async-start(), calls=%async_computation.8 | async-start | bytes 7077888 | tf_op jit(solution)/shard_map/all_gather | solution.py:75
  108.9 57.8 %copy-start.9 = (bf16[2,256,768]{2,1,0:T(8,128)(2,1)S(1)}, bf16[2,256,768]{2,1,0:T(8,128)(2,1)}, u32[]{:S(2)}) copy-start(bf16[2,256,768]{2,1,0:T(8,128)(2,1)} %param.15) | copy-start | bytes 2359300
  109.5 59.7 %copy-start.5 = (f32[768]{0:T(1024)S(1)}, f32[768]{0:T(1024)}, u32[]{:S(2)}) copy-start(f32[768]{0:T(1024)} %param.24) | copy-start | bytes 9220
  109.5 59.7 %copy-start.6 = (f32[768]{0:T(1024)S(1)}, f32[768]{0:T(1024)}, u32[]{:S(2)}) copy-start(f32[768]{0:T(1024)} %param.23) | copy-start | bytes 9220
  109.5 61.0 %copy-start.2 = (bf16[24,384]{1,0:T(8,128)(2,1)S(1)}, bf16[24,384]{1,0:T(8,128)(2,1)}, u32[]{:S(2)}) copy-start(bf16[24,384]{1,0:T(8,128)(2,1)} %param.25) | copy-start | bytes 55300
  109.5 99.5 %copy-start.3 = (bf16[384,24]{0,1:T(8,128)(2,1)S(1)}, bf16[384,24]{0,1:T(8,128)(2,1)}, u32[]{:S(2)}) copy-start(bf16[384,24]{0,1:T(8,128)(2,1)} %param.26) | copy-start | bytes 55300
  170.4 166.3 %reduce-scatter.5.cloned.1.call-start = ((), (), s32[]{:S(2)}) async-start(), calls=%async_computation.9 | async-start | bytes 7077888 | tf_op jit(solution)/shard_map/reduce_scatter | solution.py:82
  269.4 0.7 copy-start.10
  269.4 0.8 copy-start.11
  269.4 7.0 %copy-start.4 = (s32[1024]{0:T(1024)S(1)}, s32[1024]{0:T(1024)}, u32[]{:S(2)}) copy-start(s32[1024]{0:T(1024)} %param.19) | copy-start | bytes 12292
  269.4 70.2 %copy-start.7 = (f32[768]{0:T(1024)S(1)}, f32[768]{0:T(1024)}, u32[]{:S(2)}) copy-start(f32[768]{0:T(1024)} %param.28) | copy-start | bytes 9220
  269.4 70.2 %copy-start.8 = (f32[768]{0:T(1024)S(1)}, f32[768]{0:T(1024)}, u32[]{:S(2)}) copy-start(f32[768]{0:T(1024)} %param.27) | copy-start | bytes 9220
  271.0 13.9 %all-to-all-start.2 = ((s32[32,2,1]{1,2,0:T(1,128)}), s32[32,2,1]{1,2,0:T(1,128)S(1)}, u32[]{:S(2)}, u32[]{:S(2)}) async-start(s32[32,2,1]{1,2,0:T(1,128)} %bitcast.14), calls=%async_computation.3 | async-start | bytes 32768 | tf_op jit(solution)/shard_map/all_to_all | solution.py:101
  342.0 9.1 %all-to-all-start = ((f32[2,8,96]{2,0,1:T(2,128)}), f32[2,8,96]{2,0,1:T(2,128)S(1)}, u32[]{:S(2)}, u32[]{:S(2)}) async-start(f32[2,8,96]{2,0,1:T(2,128)} %copy.46), calls=%async_computation.1 | async-start | bytes 16384 | tf_op jit(solution)/shard_map/all_to_all | solution.py:87
  352.0 18.4 %all-to-all-start.1 = ((f32[32,2,96]{2,1,0:T(2,128)}), f32[32,2,96]{2,1,0:T(2,128)S(1)}, u32[]{:S(2)}, u32[]{:S(2)}) async-start(f32[32,2,96]{2,1,0:T(2,128)} %copy.47), calls=%async_computation.2 | async-start | bytes 65536 | tf_op jit(solution)/shard_map/all_to_all | solution.py:100
  361.6 68.9 %reduce-scatter.7.cloned.1.call-start = ((), (), s32[]{:S(2)}) async-start(), calls=%async_computation.10 | async-start | bytes 442368
  389.9 42.0 %copy-start.1 = (f32[1024,768]{1,0:T(8,128)}, f32[1024,768]{1,0:T(8,128)S(1)}, u32[]{:S(2)}) copy-start(f32[1024,768]{1,0:T(8,128)S(1)} %add_divide_fusion) | copy-start | bytes 9437188
Sparse Core Ops, SparseCore 0:
  10.6 81.0 all-gather.4
  94.3 72.3 all-gather.6
  170.6 45.7 all-gather.8
  269.6 67.1 reduce-scatter.4
  405.8 24.6 reduce-scatter.6
where the time goes:
time: 441 us; the launch traced here: 438 us
  waiting for transfers between devices  237 us (54%)
  blocking collectives  102 us (23%)
  matrix products  38.3 us (9%)
  starting transfers between devices  19.6 us (4%)
  local copies, waits for them, and re-layouts  15.8 us (4%)
  between operations  14.1 us (3%)
  other arithmetic  11.6 us (3%)
    all_gather x1, waiting for transfers between devices, local(): lax.all_gather(w_qkv, 'dp', axis=0, tiled=True)  82.2 us
    all_gather x1, waiting for transfers between devices, local(): lax.all_gather(w_out, 'dp', axis=0, tiled=True)  56.2 us
    reduce_scatter x1, waiting for transfers between devices, local(): lax.psum_scatter(terms.astype(jnp.bfloat16), 'tensor', scatter_dimension=...  50.5 us
    all_gather x1, blocking collectives, local(): lax.all_gather(w_up, 'dp', axis=0, tiled=True)  38.5 us
    all_gather x1, blocking collectives, local(): lax.all_gather(w_down, 'dp', axis=1, tiled=True)  37.3 us
    unnamed x6, waiting for transfers between devices  26.2 us
    dot_general x1, matrix products, local(): jnp.dot(act, down_full, preferred_element_type=jnp.float32)  23 us
    all_gather x1, blocking collectives, local(): recv_vals = lax.all_gather(recv_emb, 'tensor', axis=1, tiled=True)  14.8 us
  transfers between devices with their start and end apart: 8, of which 7 were waited for; matrix products, arithmetic and copies ran while one was open for 5% of the time, Pallas kernels for 0%

commit v1 on v0

v1 whole, which is shorter than its diff:
```python
import functools

import jax
import jax.numpy as jnp
from jax import lax
from jax.experimental import pallas as pl
from jax.experimental.pallas import tpu as pltpu
from jax.sharding import PartitionSpec as P

EPS = 1e-05
MESH = pl.DeviceIdType.MESH
F32 = jnp.float32
BF16 = jnp.bfloat16

L = 256
D = 768
SLAB = 384
N_Y = 4
N_Z = 8
N_X = 4
ROWS = 512


def split3(values):
    high = values.astype(BF16)
    rest = values - high.astype(F32)
    mid = rest.astype(BF16)
    low = (rest - mid.astype(F32)).astype(BF16)
    return high, mid, low


def pick(hot, values):
    parts = split3(values)
    return sum(jnp.dot(hot, part, preferred_element_type=F32) for part in parts)


class Ring:
    def __init__(self, sems, n, me, right, left, block, halves):
        self.n, self.me, self.right, self.left = n, me, right, left
        self.block, self.halves = block, halves
        self.sems = sems
        self.ids = [(sems.take(), sems.take()) for _ in range(n // 2)]

    def _at(self, offset):
        return lax.rem(self.me + offset + self.n, self.n)

    def _refs(self, step):
        last = step == self.n // 2
        out_right, out_left = self._at(-(step - 1)), self._at(step - 1)
        in_left, in_right = self._at(-step), self._at(step)
        if last:
            return (
                self.halves(out_right)[0],
                self.halves(out_left)[1],
                self.halves(in_left)[0],
                self.halves(in_right)[1],
            )
        return tuple(self.block(i) for i in (out_right, out_left, in_left, in_right))

    def start(self, step):
        to_right, to_left, _, _ = self._refs(step)
        a, b = self.ids[step - 1]
        self.sems.send(to_right, a, self.right)
        self.sems.send(to_left, b, self.left)

    def wait(self, step):
        _, _, from_left, from_right = self._refs(step)
        a, b = self.ids[step - 1]
        self.sems.arrived(from_left, a, self.right)
        self.sems.arrived(from_right, b, self.left)


class Copies:
    def __init__(self, send, recv):
        self.send_sems, self.recv_sems = send, recv
        self.count = 0
        self.started = []

    def take(self):
        self.count += 1
        return self.count - 1

    def _copy(self, src, dst, number, device):
        return pltpu.make_async_remote_copy(
            src_ref=src,
            dst_ref=dst,
            send_sem=self.send_sems.at[number],
            recv_sem=self.recv_sems.at[number],
            device_id=device,
            device_id_type=MESH,
        )

    def send(self, src, number, device, dst=None):
        copy = self._copy(src, src if dst is None else dst, number, device)
        copy.start()
        self.started.append(copy)

    def arrived(self, ref, number, device):
        self._copy(ref, ref, number, device).wait_recv()

    def finish(self):
        for copy in self.started:
            copy.wait_send()


N_COPIES = 160


def encode_kernel(
    x_ref,
    lens_ref,
    ids_ref,
    weight_ref,
    old_ref,
    wqkv_ref,
    wout_ref,
    gain_one_ref,
    shift_one_ref,
    wup_ref,
    wdown_ref,
    gain_two_ref,
    shift_two_ref,
    rot_ref,
    emb_out,
    ids_out,
    rows_out,
    rot_out,
    w_a,
    w_u,
    w_d,
    z_a,
    z_u,
    z_d,
    turned,
    old_buf,
    rot_send,
    mine_rows,
    owner_rows,
    emb_group,
    qkv,
    ctx,
    first,
    acc,
    send_sems,
    recv_sems,
    local_sems,
):
    dp = lax.axis_index("dp")
    tens = lax.axis_index("tensor")
    y, z = dp // N_Z, lax.rem(dp, N_Z)
    x, core = tens // 2, lax.rem(tens, 2)

    def at_y(i):
        return (i * N_Z + z, tens)

    def at_z(i):
        return (y * N_Z + i, tens)

    y_right, y_left = at_y(lax.rem(y + 1, N_Y)), at_y(lax.rem(y + N_Y - 1, N_Y))
    z_right, z_left = at_z(lax.rem(z + 1, N_Z)), at_z(lax.rem(z + N_Z - 1, N_Z))
    peers = [(dp, lax.rem(tens + k, 8)) for k in range(1, 8)]
    sibling = (dp, 2 * x + 1 - core)
    is_turn_self = tens == z
    turn = [(i * N_Z + tens, z) for i in range(N_Y)]

    old_copy = pltpu.make_async_copy(old_ref, old_buf, local_sems.at[0])
    old_copy.start()

    barrier = pltpu.get_barrier_semaphore()
    for device in [y_right, y_left, z_right, z_left] + peers:
        pl.semaphore_signal(barrier, inc=1, device_id=device, device_id_type=MESH)
    for i in range(N_Y):
        @pl.when(jnp.logical_not(jnp.logical_and(is_turn_self, y == i)))
        def _():
            pl.semaphore_signal(barrier, inc=1, device_id=turn[i], device_id_type=MESH)

    for s in range(3):
        z_a[z, s] = wqkv_ref[:, pl.ds(pl.multiple_of((2 * s + core) * SLAB, 128), SLAB)]
    z_a[z, 3] = wout_ref[:, pl.ds(pl.multiple_of(core * SLAB, 128), SLAB)]
    z_u[z, x] = wup_ref[...]
    z_d[z, x] = wdown_ref[...]
    ids_out[y, z] = ids_ref[...]
    for k in range(8):
        rot_send[k] = rot_ref[:, k * 96 : (k + 1) * 96]

    pl.semaphore_wait(barrier, 11 + N_Y - is_turn_self.astype(jnp.int32))

    sems = Copies(send_sems, recv_sems)

    def z_ring(buf):
        return Ring(
            sems, N_Z, z, z_right, z_left,
            lambda i: buf.at[i],
            lambda i: (buf.at[i, pl.ds(0, 2)], buf.at[i, pl.ds(2, 2)]),
        )

    def rows_of(i):
        return pl.ds(pl.multiple_of(i * 192, 64), 192)

    def y_ring(buf):
        return Ring(
            sems, N_Y, y, y_right, y_left,
            lambda i: buf.at[pl.ds(core * 4, 4), rows_of(i)],
            lambda i: (
                buf.at[pl.ds(core * 4, 2), rows_of(i)],
                buf.at[pl.ds(core * 4 + 2, 2), rows_of(i)],
            ),
        )

    za, zu, zd = z_ring(z_a), z_ring(z_u), z_ring(z_d)
    ya, yu, yd = y_ring(w_a), y_ring(w_u), y_ring(w_d)
    zi = Ring(
        sems, N_Z, z, z_right, z_left,
        lambda i: ids_out.at[y, i],
        lambda i: (ids_out.at[y, i, pl.ds(0, 8)], ids_out.at[y, i, pl.ds(8, 8)]),
    )
    yi = Ring(
        sems, N_Y, y, y_right, y_left,
        lambda i: ids_out.at[i],
        lambda i: (ids_out.at[i, pl.ds(0, 4)], ids_out.at[i, pl.ds(4, 4)]),
    )

    def same_chip(buf):
        numbers = [sems.take() for _ in range(N_Y)]

        def send(offset):
            i = lax.rem(y + offset + N_Y, N_Y)
            sems.send(buf.at[pl.ds(core * 4, 4), rows_of(i)], numbers[offset], sibling)

        def wait(offset):
            i = lax.rem(y + offset + N_Y, N_Y)
            sems.arrived(
                buf.at[pl.ds((1 - core) * 4, 4), rows_of(i)], numbers[offset], sibling
            )

        return send, wait

    sa, su, sd = same_chip(w_a), same_chip(w_u), same_chip(w_d)

    def assemble(buf, full):
        for s in range(4):
            for i in range(N_Z):
                turned[i * 24 : (i + 1) * 24, :] = buf[i, s].astype(F32)
            full[core * 4 + s, rows_of(y), :] = turned[...].astype(BF16)

    za.start(1)
    zi.start(1)
    x_numbers = [(sems.take(), sems.take()) for _ in range(3)]
    for k in range(1, 4):
        device = (dp, lax.rem(tens + 2 * k, 8))
        sems.send(z_u.at[z, x], x_numbers[k - 1][0], device)
        sems.send(z_d.at[z, x], x_numbers[k - 1][1], device)
    rot_numbers = [sems.take() for _ in range(7)]
    rot_place = pl.ds(pl.multiple_of(tens * 96, 32), 96)
    rot_out[rot_place, :] = rot_send[tens]
    for k in range(1, 8):
        other = lax.rem(tens + k, 8)
        sems.send(
            rot_send.at[other], rot_numbers[k - 1], peers[k - 1], dst=rot_out.at[rot_place]
        )
    for step in (2, 3, 4):
        za.wait(step - 1)
        za.start(step)
        zi.wait(step - 1)
        zi.start(step)
    za.wait(4)
    zi.wait(4)
    assemble(z_a, w_a)
    ya.start(1)
    yi.start(1)
    sa[0](0)
    for k in range(1, 4):
        origin = lax.rem(x + N_X - k, N_X)
        device = (dp, lax.rem(tens + 2 * k, 8))
        sems.arrived(z_u.at[z, origin], x_numbers[k - 1][0], device)
        sems.arrived(z_d.at[z, origin], x_numbers[k - 1][1], device)
    zu.start(1)
    zd.start(1)
    ya.wait(1)
    ya.start(2)
    yi.wait(1)
    yi.start(2)
    sa[0](1)
    sa[0](3)
    for step in (2, 3, 4):
        zu.wait(step - 1)
        zu.start(step)
        zd.wait(step - 1)
        zd.start(step)
    zu.wait(4)
    assemble(z_u, w_u)
    yu.start(1)
    su[0](0)
    zd.wait(4)
    assemble(z_d, w_d)
    yd.start(1)
    sd[0](0)
    ya.wait(2)
    sa[0](2)
    yi.wait(2)

    old_copy.wait()
    n_slots = 8
    wanted = jnp.concatenate([ids_out[i, tens] for i in range(N_Y)], axis=0)
    owners = jnp.floor(wanted * (1.0 / 1024))
    lists = wanted - owners * 1024.0
    own = (owners == dp.astype(F32)).astype(F32)
    one = lax.broadcasted_iota(jnp.int32, (64, 64), 0)
    two = lax.broadcasted_iota(jnp.int32, (64, 64), 1)
    earlier = ((one > two) & (one // 16 == two // 16)).astype(BF16)
    rank = jnp.dot(earlier, own.astype(BF16), preferred_element_type=F32)
    hots = []
    for r in range(2):
        named = jnp.where((own > 0.5) & (rank == float(r)), lists + 1.0, 0.0)
        named = jnp.sum(named.reshape(N_Y, 16, 128), axis=1) - 1.0
        hots.append(named)
    named = jnp.concatenate(hots, axis=0)
    places = lax.broadcasted_iota(jnp.int32, (n_slots, 1024), 1).astype(F32)
    hot = places == named[:, 0:1]
    mine_rows[:, 0:D] = pick(hot.astype(F32).astype(BF16), old_buf[...])
    mine_rows[:, D : D + 128] = jnp.broadcast_to(
        jnp.sum(jnp.where(hot, weight_ref[...], 0.0), axis=1, keepdims=True), (n_slots, 128)
    )
    turn_numbers = [sems.take() for _ in range(N_Y)]
    turn_to = [((lax.rem(y + k, N_Y)) * N_Z + tens, z) for k in range(N_Y)]
    for k in range(1, N_Y):
        sems.send(mine_rows, turn_numbers[k], turn_to[k], dst=owner_rows.at[y])
    @pl.when(jnp.logical_not(is_turn_self))
    def _():
        copy = sems._copy(mine_rows, owner_rows.at[y], turn_numbers[0], turn_to[0])
        copy.start()
        copy.wait_send()
        sems.arrived(owner_rows.at[y], turn_numbers[0], turn_to[0])

    @pl.when(is_turn_self)
    def _():
        owner_rows[y] = mine_rows[...]
    for k in range(1, N_Y):
        sems.arrived(
            owner_rows.at[lax.rem(y + N_Y - k, N_Y)], turn_numbers[k], turn_to[k]
        )
    for r in range(2):
        for i in range(N_Y):
            rows_out[tens, r * N_Y + i : r * N_Y + i + 1, :] = owner_rows[
                i, pl.ds(r * N_Y + y, 1), :
            ]
    row_numbers = [sems.take() for _ in range(7)]
    for k in range(1, 8):
        sems.send(rows_out.at[tens], row_numbers[k - 1], peers[k - 1])

    yu.wait(1)
    yu.start(2)
    su[0](1)
    su[0](3)
    yd.wait(1)
    yd.start(2)
    sd[0](1)
    sd[0](3)
    yu.wait(2)
    su[0](2)
    yd.wait(2)
    sd[0](2)
    for i in range(N_Y):
        sa[1](i)

    for c in range(2):
        for k in range(3):
            part = jnp.dot(x_ref[...], w_a[c * 4 + k], preferred_element_type=F32).astype(BF16)
            if k == 0:
                part = part * 0.125
            qkv[c * 3 + k] = part
    lane = lax.broadcasted_iota(jnp.int32, (1, 128), 1)
    low = (lane < 64).astype(F32).astype(BF16)
    halves = (low, 1 - low)
    key_at = lax.broadcasted_iota(jnp.int32, (1, L), 1)
    for p in range(2):
        keys_ok = key_at < lens_ref[2 * tens + p]
        tokens = slice(p * L, (p + 1) * L)
        for c in range(2):
            for j in range(3):
                columns = slice(j * 128, (j + 1) * 128)
                q = qkv[c * 3, tokens, columns]
                k = qkv[c * 3 + 1, tokens, columns]
                v = qkv[c * 3 + 2, tokens, columns]
                total = None
                for half in halves:
                    scores = lax.dot_general(
                        q * half, k, (((1,), (1,)), ((), ())), preferred_element_type=F32
                    )
                    scores = jnp.where(keys_ok, scores, -1e30)
                    powers = jnp.exp(scores - jnp.max(scores, axis=1, keepdims=True))
                    scale = 1.0 / jnp.sum(powers, axis=1, keepdims=True)
                    probs = (powers * scale).astype(BF16)
                    part = jnp.dot(probs, v * half, preferred_element_type=F32)
                    total = part if total is None else total + part
                ctx[tokens, c * SLAB + j * 128 : c * SLAB + (j + 1) * 128] = total.astype(BF16)
    for b in range(2):
        tokens = slice(b * L, (b + 1) * L)
        mixed = jnp.concatenate(
            [
                jnp.dot(ctx[tokens, :], w_a[c * 4 + 3], preferred_element_type=F32)
                for c in range(2)
            ],
            axis=1,
        )
        values = x_ref[tokens, :].astype(F32) + mixed
        centered = values - jnp.mean(values, axis=1, keepdims=True)
        spread = jnp.mean(centered * centered, axis=1, keepdims=True)
        normed = centered * lax.rsqrt(spread + EPS) * gain_one_ref[...] + shift_one_ref[...]
        first[tokens, :] = normed.astype(BF16)
        acc[tokens, :] = normed.astype(BF16).astype(F32)

    for i in range(N_Y):
        su[1](i)
        sd[1](i)

    def slab(s, carry):
        for b in range(2):
            tokens = slice(b * L, (b + 1) * L)
            up = jnp.dot(first[tokens, :], w_u[s], preferred_element_type=F32)
            act = (0.5 * up * (1.0 + lax.erf(up * (0.5**0.5)))).astype(BF16)
            acc[tokens, :] += lax.dot_general(
                act, w_d[s], (((1,), (1,)), ((), ())), preferred_element_type=F32
            )
        return carry

    lax.fori_loop(0, 8, slab, 0)

    token_at = lax.broadcasted_iota(jnp.int32, (L, 1), 0)
    for p in range(2):
        length = lens_ref[2 * tens + p]
        values = acc[p * L : (p + 1) * L, :]
        centered = values - jnp.mean(values, axis=1, keepdims=True)
        spread = jnp.mean(centered * centered, axis=1, keepdims=True)
        scaled = centered * lax.rsqrt(spread + EPS)
        pooled = jnp.sum(jnp.where(token_at < length, scaled, 0.0), axis=0, keepdims=True)
        emb = pooled / length.astype(F32) * gain_two_ref[...] + shift_two_ref[...]
        emb_group[tens, p : p + 1, :] = emb

    group_numbers = [sems.take() for _ in range(7)]
    for k in range(1, 8):
        sems.send(emb_group.at[tens], group_numbers[k - 1], peers[k - 1])
    for k in range(1, 8):
        other = lax.rem(tens + 8 - k, 8)
        sems.arrived(emb_group.at[other], group_numbers[k - 1], peers[k - 1])
    for t in range(8):
        both = emb_group[t]
        @pl.when(core == 0)
        def _():
            emb_out[0, y, z, 2 * t : 2 * t + 2, :] = both[:, :SLAB]
        @pl.when(core == 1)
        def _():
            emb_out[1, y, z, 2 * t : 2 * t + 2, :] = both[:, SLAB:]
    ze = Ring(
        sems, N_Z, z, z_right, z_left,
        lambda i: emb_out.at[core, y, i],
        lambda i: (emb_out.at[core, y, i, pl.ds(0, 8)], emb_out.at[core, y, i, pl.ds(8, 8)]),
    )
    ye = Ring(
        sems, N_Y, y, y_right, y_left,
        lambda i: emb_out.at[core, i],
        lambda i: (emb_out.at[core, i, pl.ds(0, 4)], emb_out.at[core, i, pl.ds(4, 4)]),
    )
    for step in range(1, 5):
        ze.start(step)
        ze.wait(step)
    numbers = [sems.take() for _ in range(N_Y)]
    ye.start(1)
    sems.send(emb_out.at[core, y], numbers[0], sibling)
    ye.wait(1)
    ye.start(2)
    for k in (1, 3):
        sems.send(emb_out.at[core, lax.rem(y + k, N_Y)], numbers[k], sibling)
    ye.wait(2)
    sems.send(emb_out.at[core, lax.rem(y + 2, N_Y)], numbers[2], sibling)
    for k in range(N_Y):
        sems.arrived(emb_out.at[1 - core, lax.rem(y + k, N_Y)], numbers[k], sibling)

    for k in range(1, 8):
        origin = lax.rem(tens + 8 - k, 8)
        place = pl.ds(pl.multiple_of(origin * 96, 32), 96)
        sems.arrived(rot_out.at[place], rot_numbers[k - 1], peers[k - 1])
        sems.arrived(rows_out.at[origin], row_numbers[k - 1], peers[k - 1])
    sems.finish()


def finish_kernel(emb_ref, ids_ref, rows_ref, rot_ref, weight_ref, old_ref, rotated_ref, centroids_ref, ids_row):
    step = pl.program_id(0)
    dp = lax.axis_index("dp")

    @pl.when(step == 0)
    def _():
        ids_row[...] = jnp.transpose(ids_ref[...])[0:8, :]
        ids = ids_ref[pl.ds(pl.multiple_of(dp * 16, 16), 16), :]
        owners = jnp.floor(ids * (1.0 / 1024))
        owner_y = jnp.floor(owners * (1.0 / N_Z))
        owner_z = owners - owner_y * N_Z
        one = lax.broadcasted_iota(jnp.int32, (16, 16), 0)
        two = lax.broadcasted_iota(jnp.int32, (16, 16), 1)
        owners_row = jnp.sum(jnp.where(one == two, owners[:, 0:16], 0.0), axis=0, keepdims=True)
        rank = jnp.sum(
            ((owners[:, 0:16] == owners_row) & (two < one)).astype(F32), axis=1, keepdims=True
        )
        place = owner_z * 8.0 + rank * N_Y + owner_y
        spots = lax.broadcasted_iota(jnp.int32, (16, 64), 1).astype(F32)
        hot = (place[:, 0:64] == spots).astype(F32).astype(BF16)
        old = pick(hot, rows_ref[...])
        same = ids[:, 0:1] == ids_row[0:1, :]
        counts = jnp.sum(same.astype(F32), axis=1, keepdims=True)
        same = same.astype(F32).astype(BF16)
        weight = old[:, D : D + 1]
        result = None
        for h in range(2):
            sums = pick(same, emb_ref[h])
            centroids = (weight * old[:, h * SLAB : (h + 1) * SLAB] + sums) / (weight + counts)
            resid = emb_ref[h, pl.ds(pl.multiple_of(dp * 16, 16), 16), :] - centroids
            part = jnp.dot(
                resid,
                rot_ref[h * SLAB : (h + 1) * SLAB, :],
                precision=lax.Precision.HIGHEST,
                preferred_element_type=F32,
            )
            result = part if result is None else result + part
        rotated_ref[...] = result

    one = lax.broadcasted_iota(jnp.int32, (128, 128), 0)
    two = lax.broadcasted_iota(jnp.int32, (128, 128), 1)
    weight = jnp.sum(
        jnp.where(one == two, weight_ref[pl.ds(step, 1), :], 0.0), axis=1, keepdims=True
    )
    number = lax.broadcasted_iota(jnp.int32, (128, ROWS), 0) + dp * 1024 + step * 128
    hot = number.astype(F32) == ids_row[0:1, :]
    counts = jnp.sum(hot.astype(F32), axis=1, keepdims=True)
    hot = hot.astype(F32).astype(BF16)
    for h in range(2):
        columns = slice(h * SLAB, (h + 1) * SLAB)
        sums = pick(hot, emb_ref[h])
        centroids_ref[:, columns] = (weight * old_ref[:, columns] + sums) / (weight + counts)


VMEM = pl.BlockSpec(memory_space=pltpu.VMEM)
SMEM = pl.BlockSpec(memory_space=pltpu.SMEM)
ANY = pl.BlockSpec(memory_space=pl.ANY)


def local(
    hidden,
    lengths,
    owner_of,
    list_local,
    old_weight,
    old_centroids,
    w_qkv,
    w_out,
    gain_one,
    shift_one,
    w_up,
    w_down,
    gain_two,
    shift_two,
    rotation,
):
    lists = owner_of[:, 0] * 1024 + list_local
    ids = jnp.broadcast_to(lists.astype(F32)[:, None], (16, 128))
    weight = old_weight.astype(F32)
    vmem = pltpu.VMEM
    emb, ids, rows, rot = pl.pallas_call(
        encode_kernel,
        out_shape=(
            jax.ShapeDtypeStruct((2, N_Y, N_Z, 16, SLAB), F32),
            jax.ShapeDtypeStruct((N_Y, N_Z, 16, 128), F32),
            jax.ShapeDtypeStruct((8, 8, D + 128), F32),
            jax.ShapeDtypeStruct((D, 96), F32),
        ),
        in_specs=[VMEM, SMEM, VMEM, VMEM, ANY] + [VMEM] * 9,
        out_specs=(VMEM,) * 4,
        scratch_shapes=[
            vmem((8, D, SLAB), BF16),
            vmem((8, D, SLAB), BF16),
            vmem((8, D, SLAB), BF16),
            vmem((N_Z, 4, 24, SLAB), BF16),
            vmem((N_Z, 4, 24, SLAB), BF16),
            vmem((N_Z, 4, 24, SLAB), BF16),
            vmem((192, SLAB), F32),
            vmem((1024, D), F32),
            vmem((8, 96, 96), F32),
            vmem((8, D + 128), F32),
            vmem((N_Y, 8, D + 128), F32),
            vmem((8, 2, D), F32),
            vmem((6, ROWS, SLAB), BF16),
            vmem((ROWS, D), BF16),
            vmem((ROWS, D), BF16),
            vmem((ROWS, D), F32),
            pltpu.SemaphoreType.DMA((N_COPIES,)),
            pltpu.SemaphoreType.DMA((N_COPIES,)),
            pltpu.SemaphoreType.DMA((1,)),
        ],
        compiler_params=pltpu.CompilerParams(
            collective_id=0, has_side_effects=True, vmem_limit_bytes=50 * 2**20
        ),
    )(
        hidden.reshape(ROWS, D),
        lengths,
        ids,
        weight.reshape(1, 1024),
        old_centroids,
        w_qkv,
        w_out,
        gain_one.reshape(1, D),
        shift_one.reshape(1, D),
        w_up,
        w_down.T,
        gain_two.reshape(1, D),
        shift_two.reshape(1, D),
        rotation,
    )
    whole = lambda *shape: pl.BlockSpec(shape, lambda i: (0,) * len(shape))
    return pl.pallas_call(
        finish_kernel,
        grid=(8,),
        out_shape=(
            jax.ShapeDtypeStruct((16, 96), F32),
            jax.ShapeDtypeStruct((1024, D), F32),
        ),
        in_specs=[
            whole(2, ROWS, SLAB),
            whole(ROWS, 128),
            whole(64, D + 128),
            whole(D, 96),
            whole(8, 128),
            pl.BlockSpec((128, D), lambda i: (i, 0)),
        ],
        out_specs=(whole(16, 96), pl.BlockSpec((128, D), lambda i: (i, 0))),
        scratch_shapes=[vmem((8, ROWS), F32)],
        compiler_params=pltpu.CompilerParams(vmem_limit_bytes=40 * 2**20),
    )(
        emb.reshape(2, ROWS, SLAB),
        ids.reshape(ROWS, 128),
        rows.reshape(64, D + 128),
        rot,
        weight.reshape(8, 128),
        old_centroids,
    )


def solution(mesh):
    return jax.shard_map(
        local,
        mesh=mesh,
        in_specs=(
            P(("dp", "tensor"), None, None),
            P("dp"),
            P("dp", None),
            P("dp"),
            P("dp"),
            P("dp", None),
            P("dp", None),
            P("dp", None),
            P(),
            P(),
            P("dp", "tensor"),
            P("tensor", "dp"),
            P(),
            P(),
            P("tensor", None),
        ),
        out_specs=(P("dp", "tensor"), P("dp", None)),
        check_vma=False,
    )
```

time: 441 us -> 162 us (0.37)
  waiting for transfers between devices: 237 us -> 0 us
  Pallas kernels: 0 us -> 151 us
  blocking collectives: 102 us -> 0 us
  matrix products: 38.3 us -> 0 us
  starting transfers between devices: 19.6 us -> 0 us
  between operations: 14.1 us -> 0.67 us
  other arithmetic: 11.6 us -> 1.52 us
  local copies, waits for them, and re-layouts: 15.8 us -> 8.83 us
    pallas_call x0 -> x2, Pallas kernels: none -> 151 us  [the longest x1 143 us: local(): pl.pallas_call(encode_kernel, out_shape=(jax.ShapeDtypeStruct((2, N_Y, N_...]
    all_gather x3 -> x0, waiting for transfers between devices: 138 us -> none  [the longest x1 82.2 us: local(): lax.all_gather(w_qkv, 'dp', axis=0, tiled=True)]
    all_gather x3 -> x0, blocking collectives: 90.6 us -> none  [the longest x1 38.5 us: local(): lax.all_gather(w_up, 'dp', axis=0, tiled=True)]
    reduce_scatter x1 -> x0, waiting for transfers between devices: 50.5 us -> none  [local(): lax.psum_scatter(terms.astype(jnp.bfloat16), 'tensor', scatter_dimension=...]
    dot_general x9 -> x0, matrix products: 36.7 us -> none  [the longest x1 23 us: local(): jnp.dot(act, down_full, preferred_element_type=jnp.float32)]
    unnamed x6 -> x0, waiting for transfers between devices: 26.2 us -> none
    all_to_all x3 -> x0, waiting for transfers between devices: 21.8 us -> none  [the longest x1 8.7 us: local(): lax.all_to_all(send_emb, 'dp', split_axis=0, concat_axis=0, tiled=True)]
    all_to_all x3 -> x0, starting transfers between devices: 19.4 us -> none  [the longest x1 9.58 us: local(): lax.all_to_all(send_emb, 'dp', split_axis=0, concat_axis=0, tiled=True)]
  transfers between devices with their start and end apart: 8 -> 0, of which waited for: 7 -> 0; matrix products, arithmetic and copies ran while one was open for 5% -> 0% of each run, Pallas kernels for 0% -> 0%
where the time goes in v1:
time: 162 us
  Pallas kernels  151 us (93%)
  local copies, waits for them, and re-layouts  8.83 us (5%)
    pallas_call x1, Pallas kernels, local(): pl.pallas_call(encode_kernel, out_shape=(jax.ShapeDtypeStruct((2, N_Y, N_...  143 us
    pallas_call x1, Pallas kernels, local(): pl.pallas_call(finish_kernel, grid=(8,), out_shape=(jax.ShapeDtypeStruct(...  7.85 us
    unnamed x16, local copies, waits for them, and re-layouts  5.86 us

profile of v1, /device:TPU:1, one launch (start us, length us, event | category | flops | bytes accessed | tf_op | source)
XLA Modules:
  0.0 162.0 jit_solution(3243684480154846831)
XLA Ops:
  0.6 0.0 copy-start
  0.6 0.8 fusion
  1.5 0.8 reshape.39.gain_one_ref
  2.3 0.7 reshape.40.shift_one_ref
  3.0 0.7 reshape.41.gain_two_ref
  3.7 0.7 reshape.42.shift_two_ref
  4.4 0.1 broadcast_in_dim.2.ids_ref
  4.4 0.7 convert_bitcast_fusion
  5.1 0.0 copy-start.1
  5.1 1.1 copy-done.1
  6.3 0.0 copy-start.2
  6.3 1.0 copy-done.2
  7.2 0.0 copy-start.3
  7.2 0.9 copy-done.3
  8.1 0.0 copy-start.4
  8.1 0.8 copy-done.4
  8.9 0.0 copy-start.5
  8.9 0.7 copy-done.5
  9.6 0.0 copy-start.6
  9.6 0.7 copy-done.6
  10.3 0.0 copy-start.7
  10.3 0.7 copy-done.7
  11.0 143.1 %shard_map.158 = (f32[2,4,8,16,384]{4,3,2,1,0:T(8,128)S(1)}, f32[4,8,16,128]{3,2,1,0:T(8,128)S(1)}, f32[8,8,896]{2,1,0:T(8,128)S(1)}, f32[768,96]{1,0:T(8,128)S(1)}) custom-call(bf16[512,768]{1,0:T(8,128)(2,1)S(1)} %bitcast.13, s32[16]{0:T(128)S(1)} %copy-done.7, f32[16,128]{1,0:T(8,128)S(1)} %broadcast_in_dim.2.ids_ref, f32[1,1024]{1,0:T(1,128)S(1)} %bitcast.17, ...), custom_call_target="tpu_custom_call" | custom-call | tf_op jit(solution)/shard_map/pallas_call | solution.py:567
  154.1 0.0 copy-done
  154.1 7.9 %shard_map.159 = (f32[16,96]{1,0:T(8,128)}, f32[1024,768]{1,0:T(8,128)}) custom-call(f32[2,512,384]{2,1,0:T(8,128)S(1)} %bitcast.12, f32[512,128]{1,0:T(8,128)S(1)} %bitcast.14, f32[64,896]{1,0:T(8,128)S(1)} %bitcast.15, f32[768,96]{1,0:T(8,128)S(1)} %get-tuple-element.9.rot_ref, f32[8,128]{1,0:T(8,128)S(1)} %get-tuple-element.10.weight_ref, ...), custom_call_target="tpu_custom_call" | custom-call | tf_op jit(solution)/shard_map/pallas_call | solution.py:618
Async XLA Ops:
  0.6 153.5 %copy-start = (f32[1024,768]{1,0:T(8,128)S(1)}, f32[1024,768]{1,0:T(8,128)}, u32[]{:S(2)}) copy-start(f32[1024,768]{1,0:T(8,128)} %old_ref.3) | copy-start | bytes 9437188
  5.1 1.1 copy-start.1
  6.3 1.0 copy-start.2
  7.2 0.9 copy-start.3
  8.1 0.8 copy-start.4
  8.9 0.7 copy-start.5
  9.6 0.7 copy-start.6
  10.3 0.7 copy-start.7

commit v2 on v1

v2 whole, which is shorter than its diff:
```python
import functools

import jax
import jax.numpy as jnp
from jax import lax
from jax.experimental import pallas as pl
from jax.experimental.pallas import tpu as pltpu
from jax.sharding import PartitionSpec as P

EPS = 1e-05
MESH = pl.DeviceIdType.MESH
F32 = jnp.float32
BF16 = jnp.bfloat16

L = 256
D = 768
SLAB = 384
N_Y = 4
N_Z = 8
N_X = 4
ROWS = 512


def split3(values):
    high = values.astype(BF16)
    rest = values - high.astype(F32)
    mid = rest.astype(BF16)
    low = (rest - mid.astype(F32)).astype(BF16)
    return high, mid, low


def pick(hot, values):
    parts = split3(values)
    return sum(jnp.dot(hot, part, preferred_element_type=F32) for part in parts)


class Ring:
    def __init__(self, sems, n, me, right, left, parts):
        self.n, self.me, self.right, self.left = n, me, right, left
        self.parts = parts
        self.sems = sems
        self.ids = [[(sems.take(), sems.take()) for _ in range(2)] for _ in range(n // 2)]

    def _at(self, offset):
        return lax.rem(self.me + offset + self.n, self.n)

    def start(self, step, part):
        a, b = self.ids[step - 1][part]
        last = step == self.n // 2
        if not last or part == 0:
            self.sems.send(self.parts(self._at(1 - step))[part], a, self.right)
        if not last or part == 1:
            self.sems.send(self.parts(self._at(step - 1))[part], b, self.left)

    def wait(self, step, part):
        a, b = self.ids[step - 1][part]
        last = step == self.n // 2
        if not last or part == 0:
            self.sems.arrived(self.parts(self._at(-step))[part], a, self.right)
        if not last or part == 1:
            self.sems.arrived(self.parts(self._at(step))[part], b, self.left)

    def begin(self):
        for part in range(2):
            self.start(1, part)

    def advance(self, step):
        for part in range(2):
            self.wait(step, part)
            if step < self.n // 2:
                self.start(step + 1, part)


class Direct:
    def __init__(self, sems, n, me, device, block):
        self.sems, self.n, self.me, self.device, self.block = sems, n, me, device, block
        self.numbers = [sems.take() for _ in range(n)]

    def begin(self):
        offsets = sorted(range(1, self.n), key=lambda k: -min(k, self.n - k))
        for k in offsets:
            i = lax.rem(self.me + k, self.n)
            self.sems.send(self.block(self.me), self.numbers[k], self.device(i))

    def done(self):
        for k in range(1, self.n):
            i = lax.rem(self.me + self.n - k, self.n)
            self.sems.arrived(self.block(i), self.numbers[k], self.device(i))


class Copies:
    def __init__(self, send, recv):
        self.send_sems, self.recv_sems = send, recv
        self.count = 0
        self.started = []

    def take(self):
        self.count += 1
        return self.count - 1

    def _copy(self, src, dst, number, device):
        return pltpu.make_async_remote_copy(
            src_ref=src,
            dst_ref=dst,
            send_sem=self.send_sems.at[number],
            recv_sem=self.recv_sems.at[number],
            device_id=device,
            device_id_type=MESH,
        )

    def send(self, src, number, device, dst=None):
        copy = self._copy(src, src if dst is None else dst, number, device)
        copy.start()
        self.started.append(copy)

    def arrived(self, ref, number, device):
        self._copy(ref, ref, number, device).wait_recv()

    def finish(self):
        for copy in self.started:
            copy.wait_send()
        self.started = []


N_COPIES = 288


class Spread(Ring):
    def __init__(self, sems, n, me, right, left, sibling, mine, theirs):
        super().__init__(sems, n, me, right, left, mine)
        self.sibling, self.theirs = sibling, theirs
        self.hands = [(sems.take(), sems.take()) for _ in range(n)]

    def _hand(self, offset, part):
        number = self.hands[offset % self.n][part]
        self.sems.send(self.parts(self._at(offset))[part], number, self.sibling)

    def begin_part(self, part):
        self.start(1, part)
        self._hand(0, part)

    def begin(self):
        for part in range(2):
            self.begin_part(part)

    def advance(self, step):
        for part in range(2):
            self.wait(step, part)
            if step < self.n // 2:
                self.start(step + 1, part)
                self._hand(-step, part)
            self._hand(step, part)

    def done(self):
        for offset in range(self.n):
            for part in range(2):
                i = self._at(offset)
                self.sems.arrived(self.theirs(i)[part], self.hands[offset][part], self.sibling)


def encode_kernel(
    lens_ref,
    owner_ref,
    list_ref,
    weight_ref,
    gain_one_ref,
    shift_one_ref,
    gain_two_ref,
    shift_two_ref,
    x_any,
    old_ref,
    wqkv_ref,
    wout_ref,
    wup_ref,
    wdown_ref,
    rot_ref,
    emb_out,
    ids_out,
    rows_out,
    rot_out,
    w_a,
    w_u,
    w_d,
    z_a,
    y_k,
    y_u,
    z_d,
    turned,
    x_ref,
    x_turned,
    rot_buf,
    old_buf,
    rot_send,
    mine_rows,
    owner_rows,
    emb_group,
    qkv,
    ctx,
    first,
    act,
    acc,
    send_sems,
    recv_sems,
    local_sems,
):
    dp = lax.axis_index("dp")
    tens = lax.axis_index("tensor")
    y, z = dp // N_Z, lax.rem(dp, N_Z)
    x, core = tens // 2, lax.rem(tens, 2)

    def at_y(i):
        return (i * N_Z + z, tens)

    def at_z(i):
        return (y * N_Z + i, tens)

    y_right, y_left = at_y(lax.rem(y + 1, N_Y)), at_y(lax.rem(y + N_Y - 1, N_Y))
    z_right, z_left = at_z(lax.rem(z + 1, N_Z)), at_z(lax.rem(z + N_Z - 1, N_Z))
    peers = [(dp, lax.rem(tens + k, 8)) for k in range(1, 8)]
    sibling = (dp, 2 * x + 1 - core)
    is_turn_self = tens == z
    turn = [(i * N_Z + tens, z) for i in range(N_Y)]

    barrier = pltpu.get_barrier_semaphore()
    others = [at_y(lax.rem(y + k, N_Y)) for k in range(1, N_Y)]
    others += [at_z(lax.rem(z + k, N_Z)) for k in range(1, N_Z)]
    for device in others + peers:
        pl.semaphore_signal(barrier, inc=1, device_id=device, device_id_type=MESH)
    for i in range(N_Y):
        @pl.when(jnp.logical_not(jnp.logical_and(is_turn_self, y == i)))
        def _():
            pl.semaphore_signal(barrier, inc=1, device_id=turn[i], device_id_type=MESH)

    def cut(ref, at):
        return ref.at[:, pl.ds(pl.multiple_of(at * SLAB, 128), SLAB)]

    loads = [
        (cut(wqkv_ref, core), z_a.at[z, 0]),
        (cut(wqkv_ref, 4 + core), z_a.at[z, 1]),
        (cut(wout_ref, core), z_d.at[z, 4]),
        (cut(wqkv_ref, 2 + core), y_k.at[y]),
        (wup_ref, y_u.at[y, x]),
        (wdown_ref, z_d.at[z, x]),
        (x_any, x_ref),
        (rot_ref, rot_buf),
        (old_ref, old_buf),
    ]
    loads = [
        pltpu.make_async_copy(src, dst, local_sems.at[i]) for i, (src, dst) in enumerate(loads)
    ]
    for load in loads:
        load.start()
    ids_rows = [
        jnp.full((1, 128), owner_ref[i] * 1024 + list_ref[i], jnp.int32) for i in range(16)
    ]
    ids_out[y, z] = jnp.concatenate(ids_rows, axis=0).astype(F32)
    for load in loads[:6]:
        load.wait()
    pl.semaphore_wait(barrier, 17 + N_Y - is_turn_self.astype(jnp.int32))

    sems = Copies(send_sems, recv_sems)

    def z_rows(i):
        return pl.ds(pl.multiple_of(i * 96, 32), 96)

    def y_rows(i):
        return pl.ds(pl.multiple_of(i * 192, 64), 192)

    def y_last(buf, start, count):
        half = count // 2

        def parts(c, i):
            if half:
                return [
                    buf.at[pl.ds(c * 4 + start + k, half), y_rows(i)] for k in (0, half)
                ]
            return [
                buf.at[c * 4 + start, pl.ds(pl.multiple_of(i * 192 + k, 32), 96)] for k in (0, 96)
            ]

        return Spread(
            sems, N_Y, y, y_right, y_left, sibling,
            lambda i: parts(core, i), lambda i: parts(1 - core, i),
        )

    def z_last(buf, start, count):
        half = count // 2

        def parts(c, i):
            if half:
                return [
                    buf.at[pl.ds(c * 4 + start + k, half), z_rows(i)] for k in (0, half)
                ]
            return [
                buf.at[c * 4 + start, pl.ds(pl.multiple_of(i * 96 + k, 16), 48)] for k in (0, 48)
            ]

        return Spread(
            sems, N_Z, z, z_right, z_left, sibling,
            lambda i: parts(core, i), lambda i: parts(1 - core, i),
        )

    def assemble(blocks, full, at, rows):
        for i, block in enumerate(blocks):
            turned[i * 24 : (i + 1) * 24, :] = block.astype(F32)
        full[at, rows, :] = turned[0 : 24 * len(blocks), :].astype(BF16)

    az = Direct(sems, N_Z, z, at_z, lambda i: z_a.at[i])
    ky = Direct(sems, N_Y, y, at_y, lambda i: y_k.at[i])
    uy = Direct(sems, N_Y, y, at_y, lambda i: y_u.at[i])
    iz = Direct(sems, N_Z, z, at_z, lambda i: ids_out.at[y, i])
    iy = Direct(sems, N_Y, y, at_y, lambda i: ids_out.at[i])
    dz = Ring(
        sems, N_Z, z, z_right, z_left,
        lambda i: (z_d.at[i, pl.ds(0, 2)], z_d.at[i, pl.ds(2, 3)]),
    )
    qv, o, k_z = y_last(w_a, 0, 2), y_last(w_a, 2, 1), z_last(w_a, 3, 1)
    u_z, d_y = z_last(w_u, 0, 4), y_last(w_d, 0, 4)

    az.begin()
    ky.begin()
    x_numbers = [(sems.take(), sems.take()) for _ in range(3)]
    for at, buf in enumerate((y_u.at[y, x], z_d.at[z, x])):
        for k in range(1, 4):
            sems.send(buf, x_numbers[k - 1][at], (dp, lax.rem(tens + 2 * k, 8)))

    def along_x(buf, at):
        for k in range(1, 4):
            origin = lax.rem(x + N_X - k, N_X)
            sems.arrived(
                buf.at[origin], x_numbers[k - 1][at], (dp, lax.rem(tens + 2 * k, 8))
            )

    iz.begin()
    ky.done()
    assemble([y_k[i] for i in range(N_Y)], w_a, core * 4 + 3, z_rows(z))
    k_z.begin()
    along_x(y_u.at[y], 0)
    uy.begin()
    along_x(z_d.at[z], 1)
    dz.begin()
    az.done()
    for s in range(2):
        assemble([z_a[i, s] for i in range(N_Z)], w_a, core * 4 + s, y_rows(y))
        qv.begin_part(s)
    k_z.advance(1)
    dz.advance(1)
    uy.done()
    for s in range(4):
        assemble([y_u[i, s] for i in range(N_Y)], w_u, core * 4 + s, z_rows(z))
    k_z.advance(2)
    dz.advance(2)
    u_z.begin()
    iz.done()
    iy.begin()

    for load in loads[6:]:
        load.wait()
    column = lax.broadcasted_iota(jnp.int32, (1, D), 1)
    by_z = column // 96
    by_y = (column - by_z * 96) // 24
    source = by_y * 192 + by_z * 24 + (column - by_z * 96 - by_y * 24)
    order = lax.broadcasted_iota(jnp.int32, (D, D), 0) == source
    order = order.astype(F32).astype(BF16)
    x_turned[...] = jnp.dot(x_ref[...], order, preferred_element_type=F32).astype(BF16)

    k_z.advance(3)
    dz.advance(3)
    for k in range(8):
        rot_send[k] = rot_buf[:, k * 96 : (k + 1) * 96]
    k_z.advance(4)
    dz.advance(4)
    for s in range(5):
        full, at = (w_a, core * 4 + 2) if s == 4 else (w_d, core * 4 + s)
        assemble([z_d[i, s] for i in range(N_Z)], full, at, y_rows(y))
    qv.advance(1)
    d_y.begin()
    u_z.advance(1)
    iy.done()

    n_slots = 8
    wanted = jnp.concatenate([ids_out[i, tens] for i in range(N_Y)], axis=0)
    owners = jnp.floor(wanted * (1.0 / 1024))
    lists = wanted - owners * 1024.0
    own = (owners == dp.astype(F32)).astype(F32)
    one = lax.broadcasted_iota(jnp.int32, (64, 64), 0)
    two = lax.broadcasted_iota(jnp.int32, (64, 64), 1)
    earlier = ((one > two) & (one // 16 == two // 16)).astype(BF16)
    rank = jnp.dot(earlier, own.astype(BF16), preferred_element_type=F32)
    hots = []
    for r in range(2):
        named = jnp.where((own > 0.5) & (rank == float(r)), lists + 1.0, 0.0)
        named = jnp.sum(named.reshape(N_Y, 16, 128), axis=1) - 1.0
        hots.append(named)
    named = jnp.concatenate(hots, axis=0)
    places = lax.broadcasted_iota(jnp.int32, (n_slots, 1024), 1).astype(F32)
    hot = places == named[:, 0:1]
    mine_rows[:, 0:D] = pick(hot.astype(F32).astype(BF16), old_buf[...])
    mine_rows[:, D : D + 128] = jnp.broadcast_to(
        jnp.sum(
            jnp.where(hot, weight_ref[...].astype(F32).reshape(1, 1024), 0.0),
            axis=1,
            keepdims=True,
        ),
        (n_slots, 128),
    )
    qv.advance(2)
    o.begin()
    u_z.advance(2)
    qv.done()
    k_z.done()

    turn_numbers = [sems.take() for _ in range(N_Y)]
    turn_to = [((lax.rem(y + k, N_Y)) * N_Z + tens, z) for k in range(N_Y)]
    rot_numbers = [sems.take() for _ in range(7)]
    row_numbers = [sems.take() for _ in range(7)]
    rot_place = pl.ds(pl.multiple_of(tens * 96, 32), 96)

    def send_rows_and_rotation():
        for k in range(1, N_Y):
            sems.send(mine_rows, turn_numbers[k], turn_to[k], dst=owner_rows.at[y])

        @pl.when(jnp.logical_not(is_turn_self))
        def _():
            copy = sems._copy(mine_rows, owner_rows.at[y], turn_numbers[0], turn_to[0])
            copy.start()
            copy.wait_send()

        @pl.when(is_turn_self)
        def _():
            owner_rows[y] = mine_rows[...]

        rot_out[rot_place, :] = rot_send[tens]
        for k in range(1, 8):
            other = lax.rem(tens + k, 8)
            sems.send(
                rot_send.at[other], rot_numbers[k - 1], peers[k - 1], dst=rot_out.at[rot_place]
            )

    def share_rows():
        @pl.when(jnp.logical_not(is_turn_self))
        def _():
            sems.arrived(owner_rows.at[y], turn_numbers[0], turn_to[0])

        for k in range(1, N_Y):
            sems.arrived(
                owner_rows.at[lax.rem(y + N_Y - k, N_Y)], turn_numbers[k], turn_to[k]
            )
        for r in range(2):
            for i in range(N_Y):
                rows_out[tens, r * N_Y + i : r * N_Y + i + 1, :] = owner_rows[
                    i, pl.ds(r * N_Y + y, 1), :
                ]
        for k in range(1, 8):
            sems.send(rows_out.at[tens], row_numbers[k - 1], peers[k - 1])

    def project(c):
        for at, source in ((0, x_ref), (1, x_ref), (3, x_turned)):
            part = jnp.dot(source[...], w_a[c * 4 + at], preferred_element_type=F32).astype(BF16)
            if at == 0:
                part = part * 0.125
            qkv[c * 3 + min(at, 2)] = part

    lane = lax.broadcasted_iota(jnp.int32, (1, 128), 1)
    low = (lane < 64).astype(F32).astype(BF16)
    both_halves = (low, 1 - low)
    key_at = lax.broadcasted_iota(jnp.int32, (1, L), 1)

    def attend(p, c, j):
        keys_ok = key_at < lens_ref[2 * tens + p]
        tokens = slice(p * L, (p + 1) * L)
        columns = slice(j * 128, (j + 1) * 128)
        q = qkv[c * 3, tokens, columns]
        v = qkv[c * 3 + 1, tokens, columns]
        k = qkv[c * 3 + 2, tokens, columns]
        total = None
        for half in both_halves:
            scores = lax.dot_general(
                q * half, k, (((1,), (1,)), ((), ())), preferred_element_type=F32
            )
            scores = jnp.where(keys_ok, scores, -1e30)
            powers = jnp.exp(scores - jnp.max(scores, axis=1, keepdims=True))
            scale = 1.0 / jnp.sum(powers, axis=1, keepdims=True)
            probs = (powers * scale).astype(BF16)
            part = jnp.dot(probs, v * half, preferred_element_type=F32)
            total = part if total is None else total + part
        ctx[tokens, c * SLAB + j * 128 : c * SLAB + (j + 1) * 128] = total.astype(BF16)

    def mix(b):
        tokens = slice(b * L, (b + 1) * L)
        mixed = jnp.concatenate(
            [
                jnp.dot(ctx[tokens, :], w_a[c * 4 + 2], preferred_element_type=F32)
                for c in range(2)
            ],
            axis=1,
        )
        values = x_ref[tokens, :].astype(F32) + mixed
        centered = values - jnp.mean(values, axis=1, keepdims=True)
        spread = jnp.mean(centered * centered, axis=1, keepdims=True)
        normed = centered * lax.rsqrt(spread + EPS) * gain_one_ref[...].reshape(
            1, D
        ) + shift_one_ref[...].reshape(1, D)
        normed = normed.astype(BF16)
        acc[tokens, :] = normed.astype(F32)
        first[tokens, :] = jnp.dot(normed, order, preferred_element_type=F32).astype(BF16)

    project(0)
    send_rows_and_rotation()
    project(1)
    steps = {
        3: lambda: u_z.advance(3),
        4: lambda: o.advance(1),
        6: share_rows,
        8: lambda: o.advance(2),
        9: lambda: u_z.advance(4),
        10: lambda: d_y.advance(1),
    }
    for n, (c, p, j) in enumerate(
        (c, p, j) for c in range(2) for p in range(2) for j in range(3)
    ):
        attend(p, c, j)
        if n in steps:
            steps[n]()
    o.done()
    mix(0)
    mix(1)
    u_z.done()

    def raise_slab(s, carry):
        for b in range(2):
            tokens = slice(b * L, (b + 1) * L)
            up = jnp.dot(first[tokens, :], w_u[s], preferred_element_type=F32)
            act[s, tokens, :] = (0.5 * up * (1.0 + lax.erf(up * (0.5**0.5)))).astype(BF16)
        return carry

    def lower_slab(s, carry):
        for b in range(2):
            tokens = slice(b * L, (b + 1) * L)
            acc[tokens, :] += lax.dot_general(
                act[s, tokens, :], w_d[s], (((1,), (1,)), ((), ())), preferred_element_type=F32
            )
        return carry

    lax.fori_loop(0, 8, raise_slab, 0)
    d_y.advance(2)
    d_y.done()
    lax.fori_loop(0, 8, lower_slab, 0)

    token_at = lax.broadcasted_iota(jnp.int32, (L, 1), 0)
    for p in range(2):
        length = lens_ref[2 * tens + p]
        values = acc[p * L : (p + 1) * L, :]
        centered = values - jnp.mean(values, axis=1, keepdims=True)
        spread = jnp.mean(centered * centered, axis=1, keepdims=True)
        scaled = centered * lax.rsqrt(spread + EPS)
        pooled = jnp.sum(jnp.where(token_at < length, scaled, 0.0), axis=0, keepdims=True)
        emb = pooled / length.astype(F32) * gain_two_ref[...].reshape(1, D)
        emb_group[tens, p : p + 1, :] = emb + shift_two_ref[...].reshape(1, D)

    group_numbers = [sems.take() for _ in range(7)]
    for k in range(1, 8):
        sems.send(emb_group.at[tens], group_numbers[k - 1], peers[k - 1])
    sems.finish()
    for k in range(1, 8):
        origin = lax.rem(tens + 8 - k, 8)
        place = pl.ds(pl.multiple_of(origin * 96, 32), 96)
        sems.arrived(rot_out.at[place], rot_numbers[k - 1], peers[k - 1])
        sems.arrived(rows_out.at[origin], row_numbers[k - 1], peers[k - 1])
    for k in range(1, 8):
        other = lax.rem(tens + 8 - k, 8)
        sems.arrived(emb_group.at[other], group_numbers[k - 1], peers[k - 1])
    for t in range(8):
        both = emb_group[t]
        @pl.when(core == 0)
        def _():
            emb_out[0, y, z, 2 * t : 2 * t + 2, :] = both[:, :SLAB]
        @pl.when(core == 1)
        def _():
            emb_out[1, y, z, 2 * t : 2 * t + 2, :] = both[:, SLAB:]
    ze = Direct(sems, N_Z, z, at_z, lambda i: emb_out.at[core, y, i])

    def emb_parts(c, i):
        return emb_out.at[c, i, pl.ds(0, 4)], emb_out.at[c, i, pl.ds(4, 4)]

    ye = Spread(
        sems, N_Y, y, y_right, y_left, sibling,
        lambda i: emb_parts(core, i), lambda i: emb_parts(1 - core, i),
    )
    ze.begin()
    ze.done()
    ye.begin()
    ye.advance(1)
    ye.advance(2)
    ye.done()
    sems.finish()


def finish_kernel(emb_ref, ids_ref, rows_ref, rot_ref, weight_ref, old_ref, rotated_ref, centroids_ref, ids_row):
    step = pl.program_id(0)
    dp = lax.axis_index("dp")

    @pl.when(step == 0)
    def _():
        ids_row[...] = jnp.transpose(ids_ref[...])[0:8, :]
        ids = ids_ref[pl.ds(pl.multiple_of(dp * 16, 16), 16), :]
        owners = jnp.floor(ids * (1.0 / 1024))
        owner_y = jnp.floor(owners * (1.0 / N_Z))
        owner_z = owners - owner_y * N_Z
        one = lax.broadcasted_iota(jnp.int32, (16, 16), 0)
        two = lax.broadcasted_iota(jnp.int32, (16, 16), 1)
        owners_row = jnp.sum(jnp.where(one == two, owners[:, 0:16], 0.0), axis=0, keepdims=True)
        rank = jnp.sum(
            ((owners[:, 0:16] == owners_row) & (two < one)).astype(F32), axis=1, keepdims=True
        )
        place = owner_z * 8.0 + rank * N_Y + owner_y
        spots = lax.broadcasted_iota(jnp.int32, (16, 64), 1).astype(F32)
        hot = (place[:, 0:64] == spots).astype(F32).astype(BF16)
        old = pick(hot, rows_ref[...])
        same = ids[:, 0:1] == ids_row[0:1, :]
        counts = jnp.sum(same.astype(F32), axis=1, keepdims=True)
        same = same.astype(F32).astype(BF16)
        weight = old[:, D : D + 1]
        result = None
        for h in range(2):
            sums = pick(same, emb_ref[h])
            centroids = (weight * old[:, h * SLAB : (h + 1) * SLAB] + sums) / (weight + counts)
            resid = emb_ref[h, pl.ds(pl.multiple_of(dp * 16, 16), 16), :] - centroids
            part = jnp.dot(
                resid,
                rot_ref[h * SLAB : (h + 1) * SLAB, :],
                precision=lax.Precision.HIGHEST,
                preferred_element_type=F32,
            )
            result = part if result is None else result + part
        rotated_ref[...] = result

    one = lax.broadcasted_iota(jnp.int32, (128, 128), 0)
    two = lax.broadcasted_iota(jnp.int32, (128, 128), 1)
    weight = jnp.sum(
        jnp.where(one == two, weight_ref[pl.ds(step, 1), :], 0.0), axis=1, keepdims=True
    )
    number = lax.broadcasted_iota(jnp.int32, (128, ROWS), 0) + dp * 1024 + step * 128
    hot = number.astype(F32) == ids_row[0:1, :]
    counts = jnp.sum(hot.astype(F32), axis=1, keepdims=True)
    hot = hot.astype(F32).astype(BF16)
    for h in range(2):
        columns = slice(h * SLAB, (h + 1) * SLAB)
        sums = pick(hot, emb_ref[h])
        centroids_ref[:, columns] = (weight * old_ref[:, columns] + sums) / (weight + counts)


VMEM = pl.BlockSpec(memory_space=pltpu.VMEM)
SMEM = pl.BlockSpec(memory_space=pltpu.SMEM)
ANY = pl.BlockSpec(memory_space=pl.ANY)


def local(
    hidden,
    lengths,
    owner_of,
    list_local,
    old_weight,
    old_centroids,
    w_qkv,
    w_out,
    gain_one,
    shift_one,
    w_up,
    w_down,
    gain_two,
    shift_two,
    rotation,
):
    weight = old_weight.astype(F32)
    vmem = pltpu.VMEM
    emb, ids, rows, rot = pl.pallas_call(
        encode_kernel,
        out_shape=(
            jax.ShapeDtypeStruct((2, N_Y, N_Z, 16, SLAB), F32),
            jax.ShapeDtypeStruct((N_Y, N_Z, 16, 128), F32),
            jax.ShapeDtypeStruct((8, 8, D + 128), F32),
            jax.ShapeDtypeStruct((D, 96), F32),
        ),
        in_specs=[SMEM] * 3 + [VMEM] * 5 + [ANY] * 7,
        out_specs=(VMEM,) * 4,
        scratch_shapes=[
            vmem((8, D, SLAB), BF16),
            vmem((8, D, SLAB), BF16),
            vmem((8, D, SLAB), BF16),
            vmem((N_Z, 2, 24, SLAB), BF16),
            vmem((N_Y, 24, SLAB), BF16),
            vmem((N_Y, 4, 24, SLAB), BF16),
            vmem((N_Z, 5, 24, SLAB), BF16),
            vmem((192, SLAB), F32),
            vmem((ROWS, D), BF16),
            vmem((ROWS, D), BF16),
            vmem((96, D), F32),
            vmem((1024, D), F32),
            vmem((8, 96, 96), F32),
            vmem((8, D + 128), F32),
            vmem((N_Y, 8, D + 128), F32),
            vmem((8, 2, D), F32),
            vmem((6, ROWS, SLAB), BF16),
            vmem((ROWS, D), BF16),
            vmem((ROWS, D), BF16),
            vmem((8, ROWS, SLAB), BF16),
            vmem((ROWS, D), F32),
            pltpu.SemaphoreType.DMA((N_COPIES,)),
            pltpu.SemaphoreType.DMA((N_COPIES,)),
            pltpu.SemaphoreType.DMA((9,)),
        ],
        compiler_params=pltpu.CompilerParams(
            collective_id=0, has_side_effects=True, vmem_limit_bytes=60 * 2**20
        ),
    )(
        lengths,
        owner_of.reshape(16),
        list_local,
        old_weight,
        gain_one,
        shift_one,
        gain_two,
        shift_two,
        hidden.reshape(ROWS, D),
        old_centroids,
        w_qkv,
        w_out,
        w_up,
        w_down.T,
        rotation,
    )
    whole = lambda *shape: pl.BlockSpec(shape, lambda i: (0,) * len(shape))
    return pl.pallas_call(
        finish_kernel,
        grid=(8,),
        out_shape=(
            jax.ShapeDtypeStruct((16, 96), F32),
            jax.ShapeDtypeStruct((1024, D), F32),
        ),
        in_specs=[
            whole(2, ROWS, SLAB),
            whole(ROWS, 128),
            whole(64, D + 128),
            whole(D, 96),
            whole(8, 128),
            pl.BlockSpec((128, D), lambda i: (i, 0)),
        ],
        out_specs=(whole(16, 96), pl.BlockSpec((128, D), lambda i: (i, 0))),
        scratch_shapes=[vmem((8, ROWS), F32)],
        compiler_params=pltpu.CompilerParams(vmem_limit_bytes=40 * 2**20),
    )(
        emb.reshape(2, ROWS, SLAB),
        ids.reshape(ROWS, 128),
        rows.reshape(64, D + 128),
        rot,
        weight.reshape(8, 128),
        old_centroids,
    )


def solution(mesh):
    return jax.shard_map(
        local,
        mesh=mesh,
        in_specs=(
            P(("dp", "tensor"), None, None),
            P("dp"),
            P("dp", None),
            P("dp"),
            P("dp"),
            P("dp", None),
            P("dp", None),
            P("dp", None),
            P(),
            P(),
            P("dp", "tensor"),
            P("tensor", "dp"),
            P(),
            P(),
            P("tensor", None),
        ),
        out_specs=(P("dp", "tensor"), P("dp", None)),
        check_vma=False,
    )
```

time: 162 us -> 126 us (0.78)
  Pallas kernels: 151 us -> 120 us
  local copies, waits for them, and re-layouts: 8.83 us -> 4.29 us
    pallas_call x1, Pallas kernels: 143 us -> 113 us  [local(): pl.pallas_call(encode_kernel, out_shape=(jax.ShapeDtypeStruct((2, N_Y, N_...]
    reshape x4 -> x0, local copies, waits for them, and re-layouts: 2.9 us -> none  [the longest x1 0.83 us: local(): gain_one.reshape(1, D)]
    unnamed x16 -> x10, local copies, waits for them, and re-layouts: 5.86 us -> 4.29 us
where the time goes in v2:
time: 126 us
  Pallas kernels  120 us (95%)
  local copies, waits for them, and re-layouts  4.29 us (3%)
    pallas_call x1, Pallas kernels, local(): pl.pallas_call(encode_kernel, out_shape=(jax.ShapeDtypeStruct((2, N_Y, N_...  113 us
    pallas_call x1, Pallas kernels, local(): pl.pallas_call(finish_kernel, grid=(8,), out_shape=(jax.ShapeDtypeStruct(...  7.52 us
    unnamed x10, local copies, waits for them, and re-layouts  4.29 us

profile of v2, /device:TPU:1, one launch (start us, length us, event | category | flops | bytes accessed | tf_op | source)
XLA Modules:
  0.0 126.1 jit_solution(11384997233104983032)
XLA Ops:
  0.6 0.0 copy-start
  0.6 0.8 convert_bitcast_fusion.weight_ref
  1.5 112.8 %shard_map.158 = (f32[2,4,8,16,384]{4,3,2,1,0:T(8,128)}, f32[4,8,16,128]{3,2,1,0:T(8,128)}, f32[8,8,896]{2,1,0:T(8,128)}, f32[768,96]{1,0:T(8,128)}) custom-call(s32[16]{0:T(128)} %lens_ref.1, s32[16]{0:T(128)} %bitcast.13, s32[16]{0:T(128)} %list_ref.1, s32[1024]{0:T(1024)} %weight_ref.1, f32[768]{0:T(1024)} %gain_one_ref.1, f32[768]{0:T(1024)} %shift_one_ref.1, ...), custom_call_target="tpu_custom_call" | custom-call | tf_op jit(solution)/shard_map/pallas_call | solution.py:677
  114.3 0.0 copy-done
  114.3 0.0 copy-start.1
  114.3 1.4 %copy-done.1 = f32[2,4,8,16,384]{4,3,2,1,0:T(8,128)S(1)} copy-done((f32[2,4,8,16,384]{4,3,2,1,0:T(8,128)S(1)}, f32[2,4,8,16,384]{4,3,2,1,0:T(8,128)}, u32[]{:S(2)}) %copy-start.1) | copy-done | bytes 1572888
  115.7 0.0 copy-start.2
  115.7 1.0 copy-done.2
  116.7 0.0 copy-start.3
  116.7 0.9 copy-done.3
  117.6 0.0 copy-start.4
  117.6 0.9 copy-done.4
  118.6 7.5 %shard_map.159 = (f32[16,96]{1,0:T(8,128)}, f32[1024,768]{1,0:T(8,128)}) custom-call(f32[2,512,384]{2,1,0:T(8,128)S(1)} %bitcast.8, f32[512,128]{1,0:T(8,128)S(1)} %bitcast.9, f32[64,896]{1,0:T(8,128)S(1)} %bitcast.10, f32[768,96]{1,0:T(8,128)S(1)} %copy-done.2, f32[8,128]{1,0:T(8,128)S(1)} %convert_bitcast_fusion.weight_ref, f32[1024,768]{1,0:T(8,128)S(1)} %copy-done), custom_call_target="tpu_custom_call" | custom-call | tf_op jit(solution)/shard_map/pallas_call | solution.py:734
Async XLA Ops:
  0.6 113.6 %copy-start = (f32[1024,768]{1,0:T(8,128)S(1)}, f32[1024,768]{1,0:T(8,128)}, u32[]{:S(2)}) copy-start(f32[1024,768]{1,0:T(8,128)} %old_ref.3) | copy-start | bytes 9437188
  114.3 1.4 %copy-start.1 = (f32[2,4,8,16,384]{4,3,2,1,0:T(8,128)S(1)}, f32[2,4,8,16,384]{4,3,2,1,0:T(8,128)}, u32[]{:S(2)}) copy-start(f32[2,4,8,16,384]{4,3,2,1,0:T(8,128)} %get-tuple-element.6) | copy-start | bytes 4718596
  115.7 1.0 copy-start.2
  116.7 0.9 copy-start.3
  117.6 0.9 copy-start.4

commit v3 on v2

--- a/solution.py
+++ b/solution.py
@@ -111,14 +111,26 @@
     def send(self, src, number, device, dst=None):
         copy = self._copy(src, src if dst is None else dst, number, device)
         copy.start()
-        self.started.append(copy)
+        self.started.append((None, copy.wait_send))
+
+    def send_if(self, condition, src, number, device):
+        @pl.when(condition)
+        def _():
+            self._copy(src, src, number, device).start()
+
+        self.started.append(
+            (condition, lambda: self._copy(src, src, number, device).wait_send())
+        )
 
     def arrived(self, ref, number, device):
         self._copy(ref, ref, number, device).wait_recv()
 
     def finish(self):
-        for copy in self.started:
-            copy.wait_send()
+        for condition, wait in self.started:
+            if condition is None:
+                wait()
+            else:
+                pl.when(condition)(wait)
         self.started = []
 
 
@@ -158,15 +170,59 @@
                 self.sems.arrived(self.theirs(i)[part], self.hands[offset][part], self.sibling)
 
 
+class Third:
+    def __init__(self, sems, buf, x, y, core, at_x, at_y, y_rows, sibling):
+        self.sems, self.buf, self.core, self.at_x, self.sibling = sems, buf, core, at_x, sibling
+        self.x, self.tile = x, jnp.minimum(x, 2)
+        self.along_y = Direct(
+            sems, N_Y, y, at_y, lambda i: buf.at[core, self.tile, y_rows(i)]
+        )
+        self.numbers = [sems.take() for _ in range(N_X)]
+        self.hands = [sems.take() for _ in range(N_X)]
+        self.origins = [lax.rem(x + N_X - k, N_X) for k in range(N_X)]
+        self.comes = [
+            (i < 3) & jnp.logical_not((x == 3) & (i == 2)) for i in self.origins
+        ]
+
+    def begin_x(self):
+        self.along_y.done()
+        mine = self.buf.at[self.core, self.tile]
+        for k in range(1, N_X):
+            goes = self.x < 3
+            if k == 1:
+                goes = self.x < 2
+            self.sems.send_if(goes, mine, self.numbers[k], self.at_x(lax.rem(self.x + k, N_X)))
+        self.sems.send(mine, self.hands[0], self.sibling)
+
+    def done_x(self):
+        for k in range(1, N_X):
+            ref = self.buf.at[self.core, jnp.minimum(self.origins[k], 2)]
+
+            @pl.when(self.comes[k])
+            def _():
+                self.sems.arrived(ref, self.numbers[k], self.at_x(self.origins[k]))
+
+            self.sems.send_if(self.comes[k], ref, self.hands[k], self.sibling)
+
+    def done(self):
+        self.sems.arrived(self.buf.at[1 - self.core, self.tile], self.hands[0], self.sibling)
+        for k in range(1, N_X):
+            ref = self.buf.at[1 - self.core, jnp.minimum(self.origins[k], 2)]
+
+            @pl.when(self.comes[k])
+            def _():
+                self.sems.arrived(ref, self.hands[k], self.sibling)
+
+
 def encode_kernel(
-    lens_ref,
-    owner_ref,
-    list_ref,
-    weight_ref,
-    gain_one_ref,
-    shift_one_ref,
-    gain_two_ref,
-    shift_two_ref,
+    lens_any,
+    owner_any,
+    list_any,
+    weight_any,
+    gain_one_any,
+    shift_one_any,
+    gain_two_any,
+    shift_two_any,
     x_any,
     old_ref,
     wqkv_ref,
@@ -181,13 +237,21 @@
     w_a,
     w_u,
     w_d,
+    w_k,
+    w_o,
     z_a,
-    y_k,
     y_u,
     z_d,
     turned,
+    lens_ref,
+    owner_ref,
+    list_ref,
+    weight_ref,
+    gain_one_ref,
+    shift_one_ref,
+    gain_two_ref,
+    shift_two_ref,
     x_ref,
-    x_turned,
     rot_buf,
     old_buf,
     rot_send,
@@ -214,12 +278,47 @@
     def at_z(i):
         return (y * N_Z + i, tens)
 
+    def at_x(i):
+        return (dp, 2 * i + core)
+
     y_right, y_left = at_y(lax.rem(y + 1, N_Y)), at_y(lax.rem(y + N_Y - 1, N_Y))
     z_right, z_left = at_z(lax.rem(z + 1, N_Z)), at_z(lax.rem(z + N_Z - 1, N_Z))
     peers = [(dp, lax.rem(tens + k, 8)) for k in range(1, 8)]
     sibling = (dp, 2 * x + 1 - core)
     is_turn_self = tens == z
     turn = [(i * N_Z + tens, z) for i in range(N_Y)]
+
+    third = jnp.minimum(x, 2)
+
+    def cut(ref, at, tile=None):
+        if tile is None:
+            return ref.at[:, pl.ds(pl.multiple_of(at * SLAB, 128), SLAB)]
+        return ref.at[:, pl.ds(pl.multiple_of(at * SLAB + tile * 128, 128), 128)]
+
+    loads = [
+        (cut(wqkv_ref, core), z_a.at[z, :, pl.ds(0, SLAB)]),
+        (cut(wqkv_ref, 4 + core), z_a.at[z, :, pl.ds(SLAB, SLAB)]),
+        (cut(wqkv_ref, 2 + core, third), z_a.at[z, :, pl.ds(2 * SLAB, 128)]),
+        (wup_ref, y_u.at[y, x]),
+        (wdown_ref, z_d.at[z, :, pl.ds(0, SLAB)]),
+        (cut(wout_ref, core, third), z_d.at[z, :, pl.ds(SLAB, 128)]),
+        (owner_any, owner_ref),
+        (list_any, list_ref),
+        (lens_any, lens_ref),
+        (x_any, x_ref),
+        (gain_one_any, gain_one_ref),
+        (shift_one_any, shift_one_ref),
+        (gain_two_any, gain_two_ref),
+        (shift_two_any, shift_two_ref),
+        (weight_any, weight_ref),
+        (rot_ref, rot_buf),
+        (old_ref, old_buf),
+    ]
+    loads = [
+        pltpu.make_async_copy(src, dst, local_sems.at[i]) for i, (src, dst) in enumerate(loads)
+    ]
+    for load in loads:
+        load.start()
 
     barrier = pltpu.get_barrier_semaphore()
     others = [at_y(lax.rem(y + k, N_Y)) for k in range(1, N_Y)]
@@ -231,130 +330,96 @@
         def _():
             pl.semaphore_signal(barrier, inc=1, device_id=turn[i], device_id_type=MESH)
 
-    def cut(ref, at):
-        return ref.at[:, pl.ds(pl.multiple_of(at * SLAB, 128), SLAB)]
-
-    loads = [
-        (cut(wqkv_ref, core), z_a.at[z, 0]),
-        (cut(wqkv_ref, 4 + core), z_a.at[z, 1]),
-        (cut(wout_ref, core), z_d.at[z, 4]),
-        (cut(wqkv_ref, 2 + core), y_k.at[y]),
-        (wup_ref, y_u.at[y, x]),
-        (wdown_ref, z_d.at[z, x]),
-        (x_any, x_ref),
-        (rot_ref, rot_buf),
-        (old_ref, old_buf),
-    ]
-    loads = [
-        pltpu.make_async_copy(src, dst, local_sems.at[i]) for i, (src, dst) in enumerate(loads)
-    ]
-    for load in loads:
-        load.start()
+    for load in loads[:6]:
+        load.wait()
+    pl.semaphore_wait(barrier, 17 + N_Y - is_turn_self.astype(jnp.int32))
+
+    sems = Copies(send_sems, recv_sems)
+
+    def z_rows(i):
+        return pl.ds(pl.multiple_of(i * 96, 32), 96)
+
+    def y_rows(i):
+        return pl.ds(pl.multiple_of(i * 192, 64), 192)
+
+    def y_last(buf, count):
+        half = count // 2
+
+        def parts(c, i):
+            return [buf.at[pl.ds(c * count + k, half), y_rows(i)] for k in (0, half)]
+
+        return Spread(
+            sems, N_Y, y, y_right, y_left, sibling,
+            lambda i: parts(core, i), lambda i: parts(1 - core, i),
+        )
+
+    def z_last(buf, count):
+        half = count // 2
+
+        def parts(c, i):
+            return [buf.at[pl.ds(c * count + k, half), z_rows(i)] for k in (0, half)]
+
+        return Spread(
+            sems, N_Z, z, z_right, z_left, sibling,
+            lambda i: parts(core, i), lambda i: parts(1 - core, i),
+        )
+
+    def assemble(blocks, full):
+        wide = full.shape[-1]
+        for i, block in enumerate(blocks):
+            turned[i * 24 : (i + 1) * 24, 0:wide] = block.astype(F32)
+        full[...] = turned[0 : 24 * len(blocks), 0:wide].astype(BF16)
+
+    az = Direct(sems, N_Z, z, at_z, lambda i: z_a.at[i])
+    dz = Direct(sems, N_Z, z, at_z, lambda i: z_d.at[i])
+    ux = Direct(sems, N_X, x, at_x, lambda i: y_u.at[y, i])
+    uy = Direct(sems, N_Y, y, at_y, lambda i: y_u.at[i])
+    dx = Direct(sems, N_X, x, at_x, lambda i: w_d.at[core * 4 + i, y_rows(y)])
+    iz = Direct(sems, N_Z, z, at_z, lambda i: ids_out.at[y, i])
+    iy = Direct(sems, N_Y, y, at_y, lambda i: ids_out.at[i])
+    qv, u_z, d_y = y_last(w_a, 2), z_last(w_u, 4), y_last(w_d, 4)
+    k_x = Third(sems, w_k, x, y, core, at_x, at_y, y_rows, sibling)
+    o_x = Third(sems, w_o, x, y, core, at_x, at_y, y_rows, sibling)
+
+    az.begin()
+    ux.begin()
+    dz.begin()
+    for load in loads[6:8]:
+        load.wait()
     ids_rows = [
         jnp.full((1, 128), owner_ref[i] * 1024 + list_ref[i], jnp.int32) for i in range(16)
     ]
     ids_out[y, z] = jnp.concatenate(ids_rows, axis=0).astype(F32)
-    for load in loads[:6]:
-        load.wait()
-    pl.semaphore_wait(barrier, 17 + N_Y - is_turn_self.astype(jnp.int32))
-
-    sems = Copies(send_sems, recv_sems)
-
-    def z_rows(i):
-        return pl.ds(pl.multiple_of(i * 96, 32), 96)
-
-    def y_rows(i):
-        return pl.ds(pl.multiple_of(i * 192, 64), 192)
-
-    def y_last(buf, start, count):
-        half = count // 2
-
-        def parts(c, i):
-            if half:
-                return [
-                    buf.at[pl.ds(c * 4 + start + k, half), y_rows(i)] for k in (0, half)
-                ]
-            return [
-                buf.at[c * 4 + start, pl.ds(pl.multiple_of(i * 192 + k, 32), 96)] for k in (0, 96)
-            ]
-
-        return Spread(
-            sems, N_Y, y, y_right, y_left, sibling,
-            lambda i: parts(core, i), lambda i: parts(1 - core, i),
-        )
-
-    def z_last(buf, start, count):
-        half = count // 2
-
-        def parts(c, i):
-            if half:
-                return [
-                    buf.at[pl.ds(c * 4 + start + k, half), z_rows(i)] for k in (0, half)
-                ]
-            return [
-                buf.at[c * 4 + start, pl.ds(pl.multiple_of(i * 96 + k, 16), 48)] for k in (0, 48)
-            ]
-
-        return Spread(
-            sems, N_Z, z, z_right, z_left, sibling,
-            lambda i: parts(core, i), lambda i: parts(1 - core, i),
-        )
-
-    def assemble(blocks, full, at, rows):
-        for i, block in enumerate(blocks):
-            turned[i * 24 : (i + 1) * 24, :] = block.astype(F32)
-        full[at, rows, :] = turned[0 : 24 * len(blocks), :].astype(BF16)
-
-    az = Direct(sems, N_Z, z, at_z, lambda i: z_a.at[i])
-    ky = Direct(sems, N_Y, y, at_y, lambda i: y_k.at[i])
-    uy = Direct(sems, N_Y, y, at_y, lambda i: y_u.at[i])
-    iz = Direct(sems, N_Z, z, at_z, lambda i: ids_out.at[y, i])
-    iy = Direct(sems, N_Y, y, at_y, lambda i: ids_out.at[i])
-    dz = Ring(
-        sems, N_Z, z, z_right, z_left,
-        lambda i: (z_d.at[i, pl.ds(0, 2)], z_d.at[i, pl.ds(2, 3)]),
+    iz.begin()
+    ux.done()
+    uy.begin()
+    az.done()
+    assemble(
+        [z_a[i, :, 2 * SLAB : 2 * SLAB + 128] for i in range(N_Z)],
+        w_k.at[core, third, y_rows(y)],
     )
-    qv, o, k_z = y_last(w_a, 0, 2), y_last(w_a, 2, 1), z_last(w_a, 3, 1)
-    u_z, d_y = z_last(w_u, 0, 4), y_last(w_d, 0, 4)
-
-    az.begin()
-    ky.begin()
-    x_numbers = [(sems.take(), sems.take()) for _ in range(3)]
-    for at, buf in enumerate((y_u.at[y, x], z_d.at[z, x])):
-        for k in range(1, 4):
-            sems.send(buf, x_numbers[k - 1][at], (dp, lax.rem(tens + 2 * k, 8)))
-
-    def along_x(buf, at):
-        for k in range(1, 4):
-            origin = lax.rem(x + N_X - k, N_X)
-            sems.arrived(
-                buf.at[origin], x_numbers[k - 1][at], (dp, lax.rem(tens + 2 * k, 8))
-            )
-
-    iz.begin()
-    ky.done()
-    assemble([y_k[i] for i in range(N_Y)], w_a, core * 4 + 3, z_rows(z))
-    k_z.begin()
-    along_x(y_u.at[y], 0)
-    uy.begin()
-    along_x(z_d.at[z], 1)
-    dz.begin()
-    az.done()
+    k_x.along_y.begin()
     for s in range(2):
-        assemble([z_a[i, s] for i in range(N_Z)], w_a, core * 4 + s, y_rows(y))
+        assemble(
+            [z_a[i, :, s * SLAB : (s + 1) * SLAB] for i in range(N_Z)],
+            w_a.at[core * 2 + s, y_rows(y)],
+        )
         qv.begin_part(s)
-    k_z.advance(1)
-    dz.advance(1)
     uy.done()
     for s in range(4):
-        assemble([y_u[i, s] for i in range(N_Y)], w_u, core * 4 + s, z_rows(z))
-    k_z.advance(2)
-    dz.advance(2)
+        assemble([y_u[i, s] for i in range(N_Y)], w_u.at[core * 4 + s, z_rows(z)])
     u_z.begin()
+    k_x.begin_x()
+    dz.done()
+    assemble([z_d[i, :, 0:SLAB] for i in range(N_Z)], w_d.at[core * 4 + x, y_rows(y)])
+    dx.begin()
+    assemble(
+        [z_d[i, :, SLAB : SLAB + 128] for i in range(N_Z)], w_o.at[core, third, y_rows(y)]
+    )
     iz.done()
     iy.begin()
 
-    for load in loads[6:]:
+    for load in loads[8:]:
         load.wait()
     column = lax.broadcasted_iota(jnp.int32, (1, D), 1)
     by_z = column // 96
@@ -362,19 +427,10 @@
     source = by_y * 192 + by_z * 24 + (column - by_z * 96 - by_y * 24)
     order = lax.broadcasted_iota(jnp.int32, (D, D), 0) == source
     order = order.astype(F32).astype(BF16)
-    x_turned[...] = jnp.dot(x_ref[...], order, preferred_element_type=F32).astype(BF16)
-
-    k_z.advance(3)
-    dz.advance(3)
     for k in range(8):
         rot_send[k] = rot_buf[:, k * 96 : (k + 1) * 96]
-    k_z.advance(4)
-    dz.advance(4)
-    for s in range(5):
-        full, at = (w_a, core * 4 + 2) if s == 4 else (w_d, core * 4 + s)
-        assemble([z_d[i, s] for i in range(N_Z)], full, at, y_rows(y))
     qv.advance(1)
-    d_y.begin()
+    o_x.along_y.begin()
     u_z.advance(1)
     iy.done()
 
@@ -405,10 +461,12 @@
         (n_slots, 128),
     )
     qv.advance(2)
-    o.begin()
-    u_z.advance(2)
+    k_x.done_x()
+    dx.done()
+    d_y.begin()
+    o_x.begin_x()
     qv.done()
-    k_z.done()
+    k_x.done()
 
     turn_numbers = [sems.take() for _ in range(N_Y)]
     turn_to = [((lax.rem(y + k, N_Y)) * N_Z + tens, z) for k in range(N_Y)]
@@ -455,11 +513,14 @@
             sems.send(rows_out.at[tens], row_numbers[k - 1], peers[k - 1])
 
     def project(c):
-        for at, source in ((0, x_ref), (1, x_ref), (3, x_turned)):
-            part = jnp.dot(source[...], w_a[c * 4 + at], preferred_element_type=F32).astype(BF16)
+        for at in range(2):
+            part = jnp.dot(x_ref[...], w_a[c * 2 + at], preferred_element_type=F32).astype(BF16)
             if at == 0:
                 part = part * 0.125
-            qkv[c * 3 + min(at, 2)] = part
+            qkv[c * 3 + at] = part
+        for j in range(3):
+            part = jnp.dot(x_ref[...], w_k[c, j], preferred_element_type=F32).astype(BF16)
+            qkv[c * 3 + 2, :, j * 128 : (j + 1) * 128] = part
 
     lane = lax.broadcasted_iota(jnp.int32, (1, 128), 1)
     low = (lane < 64).astype(F32).astype(BF16)
@@ -490,8 +551,9 @@
         tokens = slice(b * L, (b + 1) * L)
         mixed = jnp.concatenate(
             [
-                jnp.dot(ctx[tokens, :], w_a[c * 4 + 2], preferred_element_type=F32)
+                jnp.dot(ctx[tokens, :], w_o[c, j], preferred_element_type=F32)
                 for c in range(2)
+                for j in range(3)
             ],
             axis=1,
         )
@@ -505,16 +567,16 @@
         acc[tokens, :] = normed.astype(F32)
         first[tokens, :] = jnp.dot(normed, order, preferred_element_type=F32).astype(BF16)
 
+    u_z.advance(2)
     project(0)
     send_rows_and_rotation()
     project(1)
     steps = {
-        3: lambda: u_z.advance(3),
-        4: lambda: o.advance(1),
+        1: lambda: u_z.advance(3),
+        3: o_x.done_x,
         6: share_rows,
-        8: lambda: o.advance(2),
-        9: lambda: u_z.advance(4),
-        10: lambda: d_y.advance(1),
+        8: lambda: u_z.advance(4),
+        11: lambda: d_y.advance(1),
     }
     for n, (c, p, j) in enumerate(
         (c, p, j) for c in range(2) for p in range(2) for j in range(3)
@@ -522,7 +584,7 @@
         attend(p, c, j)
         if n in steps:
             steps[n]()
-    o.done()
+    o_x.done()
     mix(0)
     mix(1)
     u_z.done()
@@ -596,13 +658,13 @@
     sems.finish()
 
 
-def finish_kernel(emb_ref, ids_ref, rows_ref, rot_ref, weight_ref, old_ref, rotated_ref, centroids_ref, ids_row):
+def finish_kernel(emb_ref, ids_ref, rows_ref, rot_ref, weight_ref, old_ref, rotated_ref, centroids_ref, slot_ids, slots):
     step = pl.program_id(0)
     dp = lax.axis_index("dp")
 
     @pl.when(step == 0)
     def _():
-        ids_row[...] = jnp.transpose(ids_ref[...])[0:8, :]
+        ids_row = jnp.transpose(ids_ref[...])[0:8, :]
         ids = ids_ref[pl.ds(pl.multiple_of(dp * 16, 16), 16), :]
         owners = jnp.floor(ids * (1.0 / 1024))
         owner_y = jnp.floor(owners * (1.0 / N_Z))
@@ -619,11 +681,28 @@
         old = pick(hot, rows_ref[...])
         same = ids[:, 0:1] == ids_row[0:1, :]
         counts = jnp.sum(same.astype(F32), axis=1, keepdims=True)
-        same = same.astype(F32).astype(BF16)
+        mine = jnp.floor(ids_row * (1.0 / 1024)) == dp.astype(F32)
+        before = lax.broadcasted_iota(jnp.int32, (ROWS, ROWS), 0) < lax.broadcasted_iota(
+            jnp.int32, (ROWS, ROWS), 1
+        )
+        spot = jnp.dot(
+            mine.astype(F32).astype(BF16),
+            before.astype(F32).astype(BF16),
+            preferred_element_type=F32,
+        )
+        numbers = lax.broadcasted_iota(jnp.int32, (64, ROWS), 0).astype(F32)
+        placed = (numbers == spot[0:1, :]) & mine[0:1, :]
+        named = jnp.sum(jnp.where(placed, ids_row[0:1, :] + 1.0, 0.0), axis=1, keepdims=True)
+        named = jnp.concatenate([named - 1.0, jnp.full((64, 1), -1.0, F32)], axis=0)
+        slot_ids[...] = jnp.transpose(jnp.broadcast_to(named, (128, 128)))[0:8, :]
+        taken = jnp.concatenate([same.astype(F32), placed.astype(F32)], axis=0).astype(BF16)
         weight = old[:, D : D + 1]
         result = None
         for h in range(2):
-            sums = pick(same, emb_ref[h])
+            picked = pick(taken, emb_ref[h])
+            sums = picked[0:16, :]
+            for k, part in enumerate(split3(picked[16:80, :])):
+                slots[k * 64 : (k + 1) * 64, h * SLAB : (h + 1) * SLAB] = part
             centroids = (weight * old[:, h * SLAB : (h + 1) * SLAB] + sums) / (weight + counts)
             resid = emb_ref[h, pl.ds(pl.multiple_of(dp * 16, 16), 16), :] - centroids
             part = jnp.dot(
@@ -637,22 +716,29 @@
 
     one = lax.broadcasted_iota(jnp.int32, (128, 128), 0)
     two = lax.broadcasted_iota(jnp.int32, (128, 128), 1)
-    weight = jnp.sum(
-        jnp.where(one == two, weight_ref[pl.ds(step, 1), :], 0.0), axis=1, keepdims=True
+    weight = jnp.concatenate(
+        [
+            jnp.sum(
+                jnp.where(one == two, weight_ref[pl.ds(step * 4 + i, 1), :], 0.0),
+                axis=1,
+                keepdims=True,
+            )
+            for i in range(4)
+        ],
+        axis=0,
     )
-    number = lax.broadcasted_iota(jnp.int32, (128, ROWS), 0) + dp * 1024 + step * 128
-    hot = number.astype(F32) == ids_row[0:1, :]
-    counts = jnp.sum(hot.astype(F32), axis=1, keepdims=True)
-    hot = hot.astype(F32).astype(BF16)
+    number = lax.broadcasted_iota(jnp.int32, (512, 64), 0) + dp * 1024 + step * 512
+    hot = (number.astype(F32) == slot_ids[0:1, 0:64]).astype(F32)
+    counts = jnp.sum(hot, axis=1, keepdims=True)
+    hot = jnp.concatenate([hot, hot, hot], axis=1).astype(BF16)
     for h in range(2):
         columns = slice(h * SLAB, (h + 1) * SLAB)
-        sums = pick(hot, emb_ref[h])
+        sums = jnp.dot(hot, slots[:, columns], preferred_element_type=F32)
         centroids_ref[:, columns] = (weight * old_ref[:, columns] + sums) / (weight + counts)
 
 
 VMEM = pl.BlockSpec(memory_space=pltpu.VMEM)
-SMEM = pl.BlockSpec(memory_space=pltpu.SMEM)
-ANY = pl.BlockSpec(memory_space=pl.ANY)
+HBM = pl.BlockSpec(memory_space=pltpu.HBM)
 
 
 def local(
@@ -682,18 +768,26 @@
             jax.ShapeDtypeStruct((8, 8, D + 128), F32),
             jax.ShapeDtypeStruct((D, 96), F32),
         ),
-        in_specs=[SMEM] * 3 + [VMEM] * 5 + [ANY] * 7,
+        in_specs=[HBM] * 15,
         out_specs=(VMEM,) * 4,
         scratch_shapes=[
+            vmem((4, D, SLAB), BF16),
             vmem((8, D, SLAB), BF16),
             vmem((8, D, SLAB), BF16),
-            vmem((8, D, SLAB), BF16),
-            vmem((N_Z, 2, 24, SLAB), BF16),
-            vmem((N_Y, 24, SLAB), BF16),
+            vmem((2, 3, D, 128), BF16),
+            vmem((2, 3, D, 128), BF16),
+            vmem((N_Z, 24, 2 * SLAB + 128), BF16),
             vmem((N_Y, 4, 24, SLAB), BF16),
-            vmem((N_Z, 5, 24, SLAB), BF16),
+            vmem((N_Z, 24, SLAB + 128), BF16),
             vmem((192, SLAB), F32),
-            vmem((ROWS, D), BF16),
+            pltpu.SMEM((16,), jnp.int32),
+            pltpu.SMEM((16,), jnp.int32),
+            pltpu.SMEM((16,), jnp.int32),
+            vmem((1024,), jnp.int32),
+            vmem((D,), F32),
+            vmem((D,), F32),
+            vmem((D,), F32),
+            vmem((D,), F32),
             vmem((ROWS, D), BF16),
             vmem((96, D), F32),
             vmem((1024, D), F32),
@@ -708,7 +802,7 @@
             vmem((ROWS, D), F32),
             pltpu.SemaphoreType.DMA((N_COPIES,)),
             pltpu.SemaphoreType.DMA((N_COPIES,)),
-            pltpu.SemaphoreType.DMA((9,)),
+            pltpu.SemaphoreType.DMA((17,)),
         ],
         compiler_params=pltpu.CompilerParams(
             collective_id=0, has_side_effects=True, vmem_limit_bytes=60 * 2**20
@@ -733,7 +827,7 @@
     whole = lambda *shape: pl.BlockSpec(shape, lambda i: (0,) * len(shape))
     return pl.pallas_call(
         finish_kernel,
-        grid=(8,),
+        grid=(2,),
         out_shape=(
             jax.ShapeDtypeStruct((16, 96), F32),
             jax.ShapeDtypeStruct((1024, D), F32),
@@ -744,11 +838,11 @@
             whole(64, D + 128),
             whole(D, 96),
             whole(8, 128),
-            pl.BlockSpec((128, D), lambda i: (i, 0)),
+            pl.BlockSpec((512, D), lambda i: (i, 0)),
         ],
-        out_specs=(whole(16, 96), pl.BlockSpec((128, D), lambda i: (i, 0))),
-        scratch_shapes=[vmem((8, ROWS), F32)],
-        compiler_params=pltpu.CompilerParams(vmem_limit_bytes=40 * 2**20),
+        out_specs=(whole(16, 96), pl.BlockSpec((512, D), lambda i: (i, 0))),
+        scratch_shapes=[vmem((8, 128), F32), vmem((192, D), BF16)],
+        compiler_params=pltpu.CompilerParams(vmem_limit_bytes=60 * 2**20),
     )(
         emb.reshape(2, ROWS, SLAB),
         ids.reshape(ROWS, 128),

time: 126 us -> 115 us (0.913)
  Pallas kernels: 120 us -> 113 us
  local copies, waits for them, and re-layouts: 4.29 us -> 0 us
    pallas_call x1, Pallas kernels: 113 us -> 107 us  [local(): pl.pallas_call(encode_kernel, out_shape=(jax.ShapeDtypeStruct((2, N_Y, N_...]
    unnamed x10 -> x0, local copies, waits for them, and re-layouts: 4.29 us -> none
    pallas_call x1, Pallas kernels: 7.52 us -> 5.86 us  [local(): pl.pallas_call(finish_kernel, grid=(2,), out_shape=(jax.ShapeDtypeStruct(...]
where the time goes in v3:
time: 115 us
  Pallas kernels  113 us (98%)
  other arithmetic  1.28 us (1%)
    pallas_call x1, Pallas kernels, local(): pl.pallas_call(encode_kernel, out_shape=(jax.ShapeDtypeStruct((2, N_Y, N_...  107 us
    pallas_call x1, Pallas kernels, local(): pl.pallas_call(finish_kernel, grid=(2,), out_shape=(jax.ShapeDtypeStruct(...  5.86 us

profile of v3, /device:TPU:1, one launch (start us, length us, event | category | flops | bytes accessed | tf_op | source)
XLA Modules:
  0.0 115.1 jit_solution(1188983646648468075)
XLA Ops:
  0.6 1.3 %convert_bitcast_fusion.weight_ref = f32[8,128]{1,0:T(8,128)} fusion(s32[1024]{0:T(1024)} %weight_any.1), kind=kLoop, calls=%fused_computation | loop fusion | flops 1024 | bytes 8192 | tf_op jit(solution)/shard_map/reshape | solution.py:851
  1.9 107.3 %shard_map.158 = (f32[2,4,8,16,384]{4,3,2,1,0:T(8,128)}, f32[4,8,16,128]{3,2,1,0:T(8,128)}, f32[8,8,896]{2,1,0:T(8,128)}, f32[768,96]{1,0:T(8,128)}) custom-call(s32[16]{0:T(128)} %lens_any.1, s32[16]{0:T(128)} %bitcast.13, s32[16]{0:T(128)} %list_any.1, s32[1024]{0:T(1024)} %weight_any.1, f32[768]{0:T(1024)} %gain_one_any.1, f32[768]{0:T(1024)} %shift_one_any.1, ...), custom_call_target="tpu_custom_call" | custom-call | tf_op jit(solution)/shard_map/pallas_call | solution.py:763
  109.2 5.9 %shard_map.159 = (f32[16,96]{1,0:T(8,128)}, f32[1024,768]{1,0:T(8,128)}) custom-call(f32[2,512,384]{2,1,0:T(8,128)} %bitcast.8, f32[512,128]{1,0:T(8,128)} %bitcast.10, f32[64,896]{1,0:T(8,128)} %bitcast.11, f32[768,96]{1,0:T(8,128)} %get-tuple-element.9.rot_ref, f32[8,128]{1,0:T(8,128)} %convert_bitcast_fusion.weight_ref, f32[1024,768]{1,0:T(8,128)} %old_ref.3), custom_call_target="tpu_custom_call" | custom-call | tf_op jit(solution)/shard_map/pallas_call | solution.py:828

commit v4 on v3

--- a/solution.py
+++ b/solution.py
@@ -163,8 +163,8 @@
                 self._hand(-step, part)
             self._hand(step, part)
 
-    def done(self):
-        for offset in range(self.n):
+    def done(self, offsets=None):
+        for offset in range(self.n) if offsets is None else offsets:
             for part in range(2):
                 i = self._at(offset)
                 self.sems.arrived(self.theirs(i)[part], self.hands[offset][part], self.sibling)
@@ -237,6 +237,7 @@
     w_a,
     w_u,
     w_d,
+    w_e,
     w_k,
     w_o,
     z_a,
@@ -375,6 +376,9 @@
     ux = Direct(sems, N_X, x, at_x, lambda i: y_u.at[y, i])
     uy = Direct(sems, N_Y, y, at_y, lambda i: y_u.at[i])
     dx = Direct(sems, N_X, x, at_x, lambda i: w_d.at[core * 4 + i, y_rows(y)])
+    ey = Direct(sems, N_Y, y, at_y, lambda i: w_e.at[core * 4 + x, y_rows(i)])
+    ex = Direct(sems, N_X, x, at_x, lambda i: w_e.at[core * 4 + i])
+    e_hand = sems.take()
     iz = Direct(sems, N_Z, z, at_z, lambda i: ids_out.at[y, i])
     iy = Direct(sems, N_Y, y, at_y, lambda i: ids_out.at[i])
     qv, u_z, d_y = y_last(w_a, 2), z_last(w_u, 4), y_last(w_d, 4)
@@ -411,8 +415,9 @@
     u_z.begin()
     k_x.begin_x()
     dz.done()
-    assemble([z_d[i, :, 0:SLAB] for i in range(N_Z)], w_d.at[core * 4 + x, y_rows(y)])
+    assemble([z_d[i, :, 0:256] for i in range(N_Z)], w_d.at[core * 4 + x, y_rows(y)])
     dx.begin()
+    assemble([z_d[i, :, 256:SLAB] for i in range(N_Z)], w_e.at[core * 4 + x, y_rows(y)])
     assemble(
         [z_d[i, :, SLAB : SLAB + 128] for i in range(N_Z)], w_o.at[core, third, y_rows(y)]
     )
@@ -431,6 +436,7 @@
         rot_send[k] = rot_buf[:, k * 96 : (k + 1) * 96]
     qv.advance(1)
     o_x.along_y.begin()
+    ey.begin()
     u_z.advance(1)
     iy.done()
 
@@ -465,6 +471,8 @@
     dx.done()
     d_y.begin()
     o_x.begin_x()
+    ey.done()
+    ex.begin()
     qv.done()
     k_x.done()
 
@@ -511,6 +519,10 @@
                 ]
         for k in range(1, 8):
             sems.send(rows_out.at[tens], row_numbers[k - 1], peers[k - 1])
+
+    def share_e():
+        ex.done()
+        sems.send(w_e.at[pl.ds(core * 4, 4)], e_hand, sibling)
 
     def project(c):
         for at in range(2):
@@ -574,6 +586,7 @@
     steps = {
         1: lambda: u_z.advance(3),
         3: o_x.done_x,
+        5: share_e,
         6: share_rows,
         8: lambda: u_z.advance(4),
         11: lambda: d_y.advance(1),
@@ -589,25 +602,33 @@
     mix(1)
     u_z.done()
 
-    def raise_slab(s, carry):
-        for b in range(2):
-            tokens = slice(b * L, (b + 1) * L)
-            up = jnp.dot(first[tokens, :], w_u[s], preferred_element_type=F32)
-            act[s, tokens, :] = (0.5 * up * (1.0 + lax.erf(up * (0.5**0.5)))).astype(BF16)
+    def raise_slabs(n, carry):
+        for s in (2 * n, 2 * n + 1):
+            for b in range(2):
+                tokens = slice(b * L, (b + 1) * L)
+                up = jnp.dot(first[tokens, :], w_u[s], preferred_element_type=F32)
+                half = 0.5 * up
+                act[s, tokens, :] = (half + half * lax.erf(up * (0.5**0.5))).astype(BF16)
         return carry
 
-    def lower_slab(s, carry):
-        for b in range(2):
-            tokens = slice(b * L, (b + 1) * L)
-            acc[tokens, :] += lax.dot_general(
-                act[s, tokens, :], w_d[s], (((1,), (1,)), ((), ())), preferred_element_type=F32
+    def lower_slabs(n, carry):
+        total = acc[...]
+        for s in (2 * n, 2 * n + 1):
+            total = total + lax.dot_general(
+                act[s, :, 0:256], w_d[s], (((1,), (1,)), ((), ())), preferred_element_type=F32
             )
+        last = jnp.concatenate([act[s, :, 256:SLAB] for s in (2 * n, 2 * n + 1)], axis=1)
+        weights = jnp.concatenate([w_e[s] for s in (2 * n, 2 * n + 1)], axis=1)
+        acc[...] = total + lax.dot_general(
+            last, weights, (((1,), (1,)), ((), ())), preferred_element_type=F32
+        )
         return carry
 
-    lax.fori_loop(0, 8, raise_slab, 0)
+    lax.fori_loop(0, 4, raise_slabs, 0)
     d_y.advance(2)
+    sems.arrived(w_e.at[pl.ds((1 - core) * 4, 4)], e_hand, sibling)
     d_y.done()
-    lax.fori_loop(0, 8, lower_slab, 0)
+    lax.fori_loop(0, 4, lower_slabs, 0)
 
     token_at = lax.broadcasted_iota(jnp.int32, (L, 1), 0)
     for p in range(2):
@@ -719,7 +740,7 @@
     weight = jnp.concatenate(
         [
             jnp.sum(
-                jnp.where(one == two, weight_ref[pl.ds(step * 4 + i, 1), :], 0.0),
+                jnp.where(one == two, weight_ref[pl.ds(step * 4 + i, 1), :].astype(F32), 0.0),
                 axis=1,
                 keepdims=True,
             )
@@ -758,7 +779,6 @@
     shift_two,
     rotation,
 ):
-    weight = old_weight.astype(F32)
     vmem = pltpu.VMEM
     emb, ids, rows, rot = pl.pallas_call(
         encode_kernel,
@@ -773,7 +793,8 @@
         scratch_shapes=[
             vmem((4, D, SLAB), BF16),
             vmem((8, D, SLAB), BF16),
-            vmem((8, D, SLAB), BF16),
+            vmem((8, D, 256), BF16),
+            vmem((8, D, 128), BF16),
             vmem((2, 3, D, 128), BF16),
             vmem((2, 3, D, 128), BF16),
             vmem((N_Z, 24, 2 * SLAB + 128), BF16),
@@ -848,7 +869,7 @@
         ids.reshape(ROWS, 128),
         rows.reshape(64, D + 128),
         rot,
-        weight.reshape(8, 128),
+        old_weight.reshape(8, 128),
         old_centroids,
     )
 

time: 115 us -> 111 us (0.965)
  Pallas kernels: 113 us -> 110 us
  other arithmetic: 1.28 us -> 0 us
    pallas_call x1, Pallas kernels: 107 us -> 105 us  [local(): pl.pallas_call(encode_kernel, out_shape=(jax.ShapeDtypeStruct((2, N_Y, N_...]
    reshape x1 -> x0, other arithmetic: 1.28 us -> none  [local(): weight.reshape(8, 128)]
where the time goes in v4:
time: 111 us
  Pallas kernels  110 us (99%)
    pallas_call x1, Pallas kernels, local(): pl.pallas_call(encode_kernel, out_shape=(jax.ShapeDtypeStruct((2, N_Y, N_...  105 us
    pallas_call x1, Pallas kernels, local(): pl.pallas_call(finish_kernel, grid=(2,), out_shape=(jax.ShapeDtypeStruct(...  5.84 us

profile of v4, /device:TPU:1, one launch (start us, length us, event | category | flops | bytes accessed | tf_op | source)
XLA Modules:
  0.0 111.0 jit_solution(14785741845211570368)
XLA Ops:
  0.6 104.5 %shard_map.158 = (f32[2,4,8,16,384]{4,3,2,1,0:T(8,128)}, f32[4,8,16,128]{3,2,1,0:T(8,128)}, f32[8,8,896]{2,1,0:T(8,128)}, f32[768,96]{1,0:T(8,128)}) custom-call(s32[16]{0:T(128)} %lens_any.1, s32[16]{0:T(128)} %bitcast.13, s32[16]{0:T(128)} %list_any.1, s32[1024]{0:T(1024)} %weight_any.1, f32[768]{0:T(1024)} %gain_one_any.1, f32[768]{0:T(1024)} %shift_one_any.1, ...), custom_call_target="tpu_custom_call" | custom-call | tf_op jit(solution)/shard_map/pallas_call | solution.py:783
  105.2 5.8 %shard_map.159 = (f32[16,96]{1,0:T(8,128)}, f32[1024,768]{1,0:T(8,128)}) custom-call(f32[2,512,384]{2,1,0:T(8,128)} %bitcast.7, f32[512,128]{1,0:T(8,128)} %bitcast.9, f32[64,896]{1,0:T(8,128)} %bitcast.10, f32[768,96]{1,0:T(8,128)} %get-tuple-element.9.rot_ref, s32[8,128]{1,0:T(8,128)} %bitcast.12, f32[1024,768]{1,0:T(8,128)} %old_ref.3), custom_call_target="tpu_custom_call" | custom-call | tf_op jit(solution)/shard_map/pallas_call | solution.py:849

commit v5 on v4

--- a/solution.py
+++ b/solution.py
@@ -421,6 +421,8 @@
     assemble(
         [z_d[i, :, SLAB : SLAB + 128] for i in range(N_Z)], w_o.at[core, third, y_rows(y)]
     )
+    o_x.along_y.begin()
+    ey.begin()
     iz.done()
     iy.begin()
 
@@ -435,8 +437,7 @@
     for k in range(8):
         rot_send[k] = rot_buf[:, k * 96 : (k + 1) * 96]
     qv.advance(1)
-    o_x.along_y.begin()
-    ey.begin()
+    o_x.begin_x()
     u_z.advance(1)
     iy.done()
 
@@ -470,7 +471,6 @@
     k_x.done_x()
     dx.done()
     d_y.begin()
-    o_x.begin_x()
     ey.done()
     ex.begin()
     qv.done()

time: 111 us -> 114 us (1.027)
  Pallas kernels: 110 us -> 113 us
    pallas_call x1, Pallas kernels: 105 us -> 107 us  [local(): pl.pallas_call(encode_kernel, out_shape=(jax.ShapeDtypeStruct((2, N_Y, N_...]
where the time goes in v5:
time: 114 us
  Pallas kernels  113 us (99%)
    pallas_call x1, Pallas kernels, local(): pl.pallas_call(encode_kernel, out_shape=(jax.ShapeDtypeStruct((2, N_Y, N_...  107 us
    pallas_call x1, Pallas kernels, local(): pl.pallas_call(finish_kernel, grid=(2,), out_shape=(jax.ShapeDtypeStruct(...  5.83 us

profile of v5, /device:TPU:1, one launch (start us, length us, event | category | flops | bytes accessed | tf_op | source)
XLA Modules:
  0.0 113.8 jit_solution(13773597814058190531)
XLA Ops:
  0.6 107.3 %shard_map.158 = (f32[2,4,8,16,384]{4,3,2,1,0:T(8,128)}, f32[4,8,16,128]{3,2,1,0:T(8,128)}, f32[8,8,896]{2,1,0:T(8,128)}, f32[768,96]{1,0:T(8,128)}) custom-call(s32[16]{0:T(128)} %lens_any.1, s32[16]{0:T(128)} %bitcast.13, s32[16]{0:T(128)} %list_any.1, s32[1024]{0:T(1024)} %weight_any.1, f32[768]{0:T(1024)} %gain_one_any.1, f32[768]{0:T(1024)} %shift_one_any.1, ...), custom_call_target="tpu_custom_call" | custom-call | tf_op jit(solution)/shard_map/pallas_call | solution.py:783
  107.9 5.8 %shard_map.159 = (f32[16,96]{1,0:T(8,128)}, f32[1024,768]{1,0:T(8,128)}) custom-call(f32[2,512,384]{2,1,0:T(8,128)} %bitcast.7, f32[512,128]{1,0:T(8,128)} %bitcast.9, f32[64,896]{1,0:T(8,128)} %bitcast.10, f32[768,96]{1,0:T(8,128)} %get-tuple-element.9.rot_ref, s32[8,128]{1,0:T(8,128)} %bitcast.12, f32[1024,768]{1,0:T(8,128)} %old_ref.3), custom_call_target="tpu_custom_call" | custom-call | tf_op jit(solution)/shard_map/pallas_call | solution.py:849
